TPU v7x, 512 devices: a whole 4x8x8 slice. The times are simulated.
512 devices in a mesh: dp: 32 (over x, z_lo, core), tensor: 16 (over z_hi, y).
Axes of the slice: x: 4, y: 8, z: 8 (z_hi: 2, z_lo: 4; z = z_hi * 4 + z_lo), core: 2. Of those that a mesh axis runs over, the one named last changes fastest.
Arguments:
- learn_input: bfloat16 [8192, 8192], P('dp', 'tensor'), may hold values from -6 to 6
- cotangent: bfloat16 [8192, 2, 1024], P('dp', None, 'tensor'), may hold values from -6 to 6
- rewards: float32 [256], P('dp'), may hold values from -6 to 6
- group_ids: int32 [256], P('dp'), may hold values from 0 to 3
- adapter_down: float32 [2, 64, 8192], P(None, None, 'tensor'), may hold values from -0.0625 to 0.0625
- adapter_up: float32 [2, 64, 1024], P(None, None, 'tensor'), may hold values from -0.12 to 0.12
- frozen_weight: bfloat16 [2, 8192, 1024], P(None, 'tensor'), may hold values from -0.0625 to 0.0625
- hidden: bfloat16 [256, 4, 8192], P('dp', None, 'tensor'), may hold values from -6 to 6
- queries: bfloat16 [256, 4, 32, 128], P('dp'), may hold values from -128 to 128
- key_cache: bfloat16 [256, 768, 8, 128], P('dp', 'tensor'), may hold values from -4 to 4
- value_cache: bfloat16 [256, 768, 8, 128], P('dp', 'tensor'), may hold values from -6 to 6
- cache_lengths: int32 [256], P('dp'), may hold values from 384 to 768, as said below
Outputs:
- updated_down: float32 [2, 64, 8192], P(None, None, 'tensor')
- updated_up: float32 [2, 64, 1024], P(None, None, 'tensor')
- attended: bfloat16 [256, 4, 4096], P('dp', None, 'tensor')
Inputs may be any that keep to these rules, and one draw needn't show every extreme that they name: `group_ids`: ids number the prompts of the 8 completions of one learner shard. `cache_lengths`: positions 0 to length - 1 of a row's cache are filled; some row has 768, some row 384.
All inputs are finite; a program needn't handle non-finite values.
Results may differ from a plain program's by a relative error of at most 0.012.
Values may be sent and summed in bfloat16 or wider, within the bound.
A program may use at most 64 MiB of HBM per device.

v0:
```python
import math

import jax
import jax.numpy as jnp
from jax import lax
from jax.sharding import PartitionSpec as P

GROUPS_DEV = 4
SEQ_LEN = 32


adapter_scale = 2.0
step_size = 0.004
masked_score = -1e30


def group_advantage(rewards, group_ids):
    member = (group_ids[:, None] == jnp.arange(GROUPS_DEV, dtype=jnp.int32)[None, :]).astype(
        jnp.float32
    )
    counts = jnp.maximum(jnp.sum(member, axis=0), 1.0)
    group_mean = jnp.sum(member * rewards[:, None], axis=0) / counts
    own_mean = jnp.sum(member * group_mean[None, :], axis=1)
    offset = rewards - own_mean
    spread = jnp.sum(member * (offset * offset)[:, None], axis=0) / counts
    own_std = jnp.sum(member * jnp.sqrt(spread)[None, :], axis=1)
    return offset / jnp.maximum(own_std, 1.0)


def shards(
    learn_input,
    cotangent,
    rewards,
    group_ids,
    adapter_down,
    adapter_up,
    frozen_weight,
    hidden,
    queries,
    key_cache,
    value_cache,
    cache_lengths,
):
    advantage = group_advantage(rewards, group_ids)
    token_weight = jnp.repeat(advantage / SEQ_LEN, SEQ_LEN)
    weighted_rows = (cotangent.astype(jnp.float32) * token_weight[:, None, None]).astype(
        jnp.bfloat16
    )
    rounded_down = adapter_down.astype(jnp.bfloat16)
    rounded_up = adapter_up.astype(jnp.bfloat16)
    local_projection = jnp.einsum(
        "td,krd->tkr", learn_input, rounded_down, preferred_element_type=jnp.float32
    )
    local_backward = jnp.einsum(
        "tkc,krc->tkr", weighted_rows, rounded_up, preferred_element_type=jnp.float32
    )
    projected_rows, reverse_pass = lax.psum((local_projection, local_backward), "tensor")
    projected_rows = projected_rows.astype(jnp.bfloat16)
    reverse_pass = reverse_pass.astype(jnp.bfloat16)
    down_gradient = adapter_scale * jnp.einsum(
        "xnu,xh->nuh", reverse_pass, learn_input, preferred_element_type=jnp.float32
    )
    up_gradient = adapter_scale * jnp.einsum(
        "nhj,nhf->hjf", projected_rows, weighted_rows, preferred_element_type=jnp.float32
    )
    total_down, total_up = lax.psum((down_gradient, up_gradient), "dp")
    updated_down = adapter_down + step_size * total_down
    updated_up = adapter_up + step_size * total_up
    roll_down = updated_down.astype(jnp.bfloat16)
    reduced_rank = jnp.einsum(
        "krd,krc->kdc",
        roll_down,
        lax.all_gather(updated_up.astype(jnp.bfloat16), "tensor", axis=2, tiled=True),
        preferred_element_type=jnp.float32,
    )
    combined_weight = (frozen_weight.astype(jnp.float32) + adapter_scale * reduced_rank).astype(
        jnp.bfloat16
    )
    row_count = hidden.shape[0]
    step_count = hidden.shape[1]
    cache_slots = key_cache.shape[1]
    key_heads = key_cache.shape[2]
    head_size = key_cache.shape[3]
    query_heads = queries.shape[2]
    per_group = query_heads // key_heads
    own_heads = query_heads // lax.axis_size("tensor")
    tensor_index = lax.axis_index("tensor")
    position = tensor_index * cache_slots + jnp.arange(cache_slots, dtype=jnp.int32)
    valid_mask = position[None, :] < cache_lengths[:, None]
    score_scale = 1.0 / math.sqrt(head_size)

    def own_slice(values):
        return lax.dynamic_slice_in_dim(values, tensor_index * own_heads, own_heads, 2)

    collected = []
    pieces = []
    for step_index in range(step_count):
        local_kv = jnp.einsum(
            "rtd,kdc->rtkc",
            hidden[:, step_index : step_index + 1],
            combined_weight,
            preferred_element_type=jnp.float32,
        )
        collected.append(lax.psum(local_kv, "tensor").astype(jnp.bfloat16))
        query_block = queries[:, step_index : step_index + 1]
        recent_kv = jnp.concatenate(collected, axis=1)
        block_steps = query_block.shape[1]
        seen_steps = recent_kv.shape[1]
        grouped = query_block.reshape(row_count, block_steps, key_heads, per_group, head_size)
        new_keys = recent_kv[:, :, 0].reshape(row_count, seen_steps, key_heads, head_size)
        new_values = recent_kv[:, :, 1].reshape(row_count, seen_steps, key_heads, head_size)
        cached = (
            jnp.einsum("rtgqd,rpgd->rtgqp", grouped, key_cache, preferred_element_type=jnp.float32)
            * score_scale
        )
        cached = jnp.where(valid_mask[:, None, None, None, :], cached, masked_score)
        block_high = jnp.max(cached, axis=-1)
        cache_weight = jnp.where(
            valid_mask[:, None, None, None, :], jnp.exp(cached - block_high[..., None]), 0.0
        )
        cache_total = jnp.sum(cache_weight, axis=-1).reshape(row_count, block_steps, query_heads)
        cache_mix = jnp.einsum(
            "rtgqp,rpgd->rtgqd",
            cache_weight.astype(jnp.bfloat16),
            value_cache,
            preferred_element_type=jnp.float32,
        )
        cache_mix = cache_mix.reshape(row_count, block_steps, query_heads, head_size)
        block_high = block_high.reshape(row_count, block_steps, query_heads)
        recent = (
            jnp.einsum("rtgqd,rjgd->rtgqj", grouped, new_keys, preferred_element_type=jnp.float32)
            * score_scale
        )
        causal = (step_index + jnp.arange(block_steps))[:, None] >= jnp.arange(seen_steps)[None, :]
        recent = jnp.where(causal[None, :, None, None, :], recent, masked_score)
        new_high = jnp.max(recent, axis=-1)
        new_weight = jnp.where(
            causal[None, :, None, None, :], jnp.exp(recent - new_high[..., None]), 0.0
        )
        new_total = jnp.sum(new_weight, axis=-1).reshape(row_count, block_steps, query_heads)
        new_mix = jnp.einsum(
            "rtgqj,rjgd->rtgqd",
            new_weight.astype(jnp.bfloat16),
            new_values,
            preferred_element_type=jnp.float32,
        )
        new_mix = new_mix.reshape(row_count, block_steps, query_heads, head_size)
        new_high = new_high.reshape(row_count, block_steps, query_heads)
        own_new_high = own_slice(new_high)
        highest = lax.pmax(jnp.maximum(block_high, new_high), "tensor")
        factor = jnp.exp(block_high - highest)
        sum_total, sum_mix = lax.psum(
            (factor * cache_total, factor[..., None] * cache_mix), "tensor"
        )
        sum_total = own_slice(sum_total)
        sum_mix = own_slice(sum_mix)
        highest = own_slice(highest)
        new_factor = jnp.exp(own_new_high - highest)
        mixed = (sum_mix + new_factor[..., None] * own_slice(new_mix)) / (
            sum_total + new_factor * own_slice(new_total)
        )[..., None]
        pieces.append(
            mixed.reshape(row_count, block_steps, own_heads * head_size).astype(jnp.bfloat16)
        )
    attended = jnp.concatenate(pieces, axis=1)
    return (updated_down, updated_up, attended)


def solution(mesh):
    return jax.shard_map(
        shards,
        mesh=mesh,
        in_specs=(
            P("dp", "tensor"),
            P("dp", None, "tensor"),
            P("dp"),
            P("dp"),
            P(None, None, "tensor"),
            P(None, None, "tensor"),
            P(None, "tensor", None),
            P("dp", None, "tensor"),
            P("dp", None, None, None),
            P("dp", "tensor", None, None),
            P("dp", "tensor", None, None),
            P("dp"),
        ),
        out_specs=(P(None, None, "tensor"), P(None, None, "tensor"), P("dp", None, "tensor")),
        check_vma=False,
    )
```

profile of v0, /device:TPU:1, one launch (start us, length us, event | category | flops | bytes accessed | tf_op | source)
XLA Modules:
  0.0 875.2 jit_solution(10592512639926457573)
XLA Ops:
  7.3 0.9 convert_reduce_fusion
  8.2 0.7 select_reduce_fusion.2
  9.0 0.7 fusion.153
  9.7 0.8 select_reduce_fusion.1
  10.4 0.8 select_reduce_fusion
  11.3 1.0 convolution_bitcast_fusion
  12.4 1.3 fusion.34
  13.6 94.3 %all-reduce.13 = (bf16[256,2,64]{0,2,1:T(8,128)(2,1)S(1)}, bf16[256,2,64]{0,2,1:T(8,128)(2,1)S(1)}) all-reduce(f32[256,2,64]{0,2,1:T(8,128)S(1)} %convolution_bitcast_fusion, f32[256,2,64]{0,2,1:T(8,128)S(1)} %fusion.34), channel_id=1, replica_groups=mesh['dp'=32,'tensor'=16] {'tensor'}, use_global_device_ids=true, to_apply=%region_5.0 | all-reduce | flops 65536 | bytes 393216 | tf_op jit(solution)/shard_map/psum | solution.py:57
  108.0 1.8 convolution_multiply_fusion
  109.9 0.6 iota_compare_fusion.3
  110.5 0.5 iota_compare_fusion.2
  111.2 141.5 %psum.115 = f32[2,64,64]{2,1,0:T(8,128)S(1)} all-reduce(f32[2,64,64]{2,1,0:T(8,128)S(1)} %convolution_multiply_fusion.8), channel_id=1, replica_groups=mesh['dp'=32,'tensor'=16] {'dp'}, use_global_device_ids=true, to_apply=%region_8.0 | all-reduce | flops 8192 | bytes 65536 | tf_op jit(solution)/shard_map/psum | solution.py:66
  252.7 0.6 fusion.152
  253.5 42.5 %all_gather.3 = bf16[2,64,1024]{1,0,2:T(2,128)(2,1)S(1)} all-gather(bf16[2,64,64]{1,0,2:T(2,128)(2,1)S(1)} %copy.181), channel_id=1, replica_groups=mesh['dp'=32,'tensor'=16] {'tensor'}, dimensions={2}, use_global_device_ids=true | all-gather | bytes 278528 | tf_op jit(solution)/shard_map/all_gather | solution.py:73
  296.0 0.7 fusion.155
  296.8 0.6 fusion.160
  297.4 0.6 fusion.158
  298.0 0.6 fusion.156
  298.6 0.6 fusion.162
  299.2 1.1 fusion.26
  300.3 1.0 fusion.28
  301.3 1.0 fusion.24
  302.4 1.3 fusion.39
  303.6 0.5 iota_compare_fusion.1
  304.6 0.9 copy.180
  305.4 0.9 copy.196
  306.3 1.5 copy.186
  307.8 0.9 copy.220
  308.7 0.9 copy.208
  309.6 1.9 fusion.22
  311.5 84.9 %all-reduce.10.cloned.1.call-done = f32[2,64,512]{2,1,0:T(8,128)} async-done(((f32[2,64,512]{2,1,0:T(8,128)}), f32[2,64,512]{2,1,0:T(8,128)}) %all-reduce.10.cloned.1.call-update) | async-done | bytes 262160 | tf_op jit(solution)/shard_map/psum | solution.py:66
  396.4 1.1 multiply_add_fusion
  397.5 0.8 add_convert_fusion
  398.4 0.4 convolution_bitcast_fusion.1
  399.5 0.4 convolution_bitcast_fusion.3
  400.3 85.6 %all-reduce.14 = (bf16[8,1,2,1024]{3,0,2,1:T(8,128)(2,1)S(1)}, bf16[8,1,2,1024]{3,0,2,1:T(8,128)(2,1)S(1)}, bf16[8,1,2,1024]{3,0,2,1:T(8,128)(2,1)S(1)}, bf16[8,1,2,1024]{3,0,2,1:T(8,128)(2,1)S(1)}) all-reduce(f32[8,1,2,1024]{3,0,2,1:T(8,128)S(1)} %convolution_bitcast_fusion.1, ...), channel_id=1, replica_groups=mesh['dp'=32,'tensor'=16] {'tensor'}, use_global_device_ids=true, to_apply=%region_32.33 | all-reduce | flops 65536 | bytes 393216 | tf_op jit(solution)/shard_map/psum | solution.py:104
  489.2 77.3 %all-reduce.4 = (f32[8,1,32]{0,2,1:T(8,128)S(1)}, f32[8,1,32]{0,2,1:T(8,128)S(1)}, f32[8,1,32]{0,2,1:T(8,128)S(1)}, f32[8,1,32]{0,2,1:T(8,128)S(1)}) all-reduce(f32[8,1,32]{0,2,1:T(8,128)S(1)} %bitcast_maximum_fusion, f32[8,1,32]{0,2,1:T(8,128)S(1)} %bitcast_maximum_fusion.1, ...), channel_id=1, replica_groups=mesh['dp'=32,'tensor'=16] {'tensor'}, use_global_device_ids=true, to_apply=%region_34.35 | all-reduce | flops 1024 | bytes 8192 | tf_op jit(solution)/shard_map/pmax | solution.py:150
  566.5 0.8 copy_multiply_fusion.2
  567.3 0.8 copy_multiply_fusion.3
  568.1 0.7 copy_multiply_fusion.1
  568.8 0.8 copy_multiply_fusion
  569.6 77.3 %all-reduce = (f32[8,1,32]{0,2,1:T(8,128)S(1)}, f32[8,1,32]{0,2,1:T(8,128)S(1)}, f32[8,1,32]{0,2,1:T(8,128)S(1)}, f32[8,1,32]{0,2,1:T(8,128)S(1)}) all-reduce(f32[8,1,32]{0,2,1:T(8,128)S(1)} %get-tuple-element.94, f32[8,1,32]{0,2,1:T(8,128)S(1)} %get-tuple-element.66, ...), channel_id=1, replica_groups=mesh['dp'=32,'tensor'=16] {'tensor'}, use_global_device_ids=true, to_apply=%region_37.38 | all-reduce | flops 1024 | bytes 8192 | tf_op jit(solution)/shard_map/psum | solution.py:152
  647.5 217.1 %all-reduce.12.cloned.1.call-done = (f32[8,1,32,128]{3,0,2,1:T(8,128)}, f32[8,1,32,128]{3,0,2,1:T(8,128)}, f32[8,1,32,128]{3,0,2,1:T(8,128)}, f32[8,1,32,128]{3,0,2,1:T(8,128)}) async-done(((f32[8,1,32,128]{3,0,2,1:T(8,128)}, f32[8,1,32,128]{3,0,2,1:T(8,128)}, f32[8,1,32,128]{3,0,2,1:T(8,128)}, f32[8,1,32,128]{3,0,2,1:T(8,128)}), (f32[8,1,32,128]{3,0,2,1:T(8,128)}, f32[8,1,32,128]{3,0,2,1:T(8,128)}, ...) | async-done | bytes 524304 | tf_op jit(solution)/shard_map/psum | solution.py:152
  864.7 0.8 fusion.116
  865.4 0.8 fusion.117
  866.2 0.8 fusion.118
  867.0 0.8 fusion.119
  867.8 0.6 copy.222
  (121 shorter events, 5.9 us)
Async XLA Ops:
  7.2 292.1 %copy-start = (bf16[8,48,8,128]{3,2,1,0:T(8,128)(2,1)S(1)}, bf16[8,48,8,128]{3,2,1,0:T(8,128)(2,1)}, u32[]{:S(2)}) copy-start(bf16[8,48,8,128]{3,2,1,0:T(8,128)(2,1)} %param.22) | copy-start | bytes 2359300
  7.2 103.8 %copy-start.4 = (bf16[256,2,64]{0,2,1:T(8,128)(2,1)S(1)}, bf16[256,2,64]{0,2,1:T(8,128)(2,1)}, u32[]{:S(2)}) copy-start(bf16[256,2,64]{0,2,1:T(8,128)(2,1)} %param.13) | copy-start | bytes 196612
  7.2 245.5 %copy-start.5 = (f32[2,64,64]{2,1,0:T(8,128)S(1)}, f32[2,64,64]{2,1,0:T(8,128)}, u32[]{:S(2)}) copy-start(f32[2,64,64]{2,1,0:T(8,128)} %param.17) | copy-start | bytes 98308
  7.2 288.8 %copy-start.11 = (bf16[8,4,512]{2,1,0:T(4,128)(2,1)S(1)}, bf16[8,4,512]{2,1,0:T(4,128)(2,1)}, u32[]{:S(2)}) copy-start(bf16[8,4,512]{2,1,0:T(4,128)(2,1)} %param.19) | copy-start | bytes 98308
  7.2 289.4 %copy-start.3 = (bf16[8,4,32,128]{3,2,1,0:T(8,128)(2,1)S(1)}, bf16[8,4,32,128]{3,2,1,0:T(8,128)(2,1)}, u32[]{:S(2)}) copy-start(bf16[8,4,32,128]{3,2,1,0:T(8,128)(2,1)} %param.20) | copy-start | bytes 786436
  7.2 289.5 %copy-start.30 = (s32[8]{0:T(128)S(1)}, s32[8]{0:T(128)}, u32[]{:S(2)}) copy-start(s32[8]{0:T(128)} %param.23) | copy-start | bytes 100
  7.2 289.6 %copy-start.31 = (bf16[8,48,8,128]{3,2,1,0:T(8,128)(2,1)S(1)}, bf16[8,48,8,128]{3,2,1,0:T(8,128)(2,1)}, u32[]{:S(2)}) copy-start(bf16[8,48,8,128]{3,2,1,0:T(8,128)(2,1)} %param.21) | copy-start | bytes 2359300
  7.2 389.1 %all-reduce.10.cloned.1.call-start = ((), (), s32[]{:S(2)}) async-start(), calls=%async_computation | async-start | bytes 524288 | tf_op jit(solution)/shard_map/psum | solution.py:66
  109.9 754.8 %all-reduce.12.cloned.1.call-start = ((), (), s32[]{:S(2)}) async-start(), calls=%async_computation.1 | async-start | bytes 1048576 | tf_op jit(solution)/shard_map/psum | solution.py:152
  296.7 1.9 copy-start.14
  296.7 1.9 copy-start.16
  296.7 1.9 copy-start.18
  296.7 1.9 copy-start.20
  296.8 5.6 copy-start.26
  298.6 3.8 copy-start.12
  299.2 4.4 copy-start.6
  301.3 96.2 %copy-start.1 = (bf16[2,512,1024]{2,1,0:T(8,128)(2,1)S(1)}, bf16[2,512,1024]{2,1,0:T(8,128)(2,1)}, u32[]{:S(2)}) copy-start(bf16[2,512,1024]{2,1,0:T(8,128)(2,1)} %param.18) | copy-start | bytes 6291460
  397.5 0.9 copy-start.2
  397.5 0.9 copy-start.25
  398.3 0.7 copy-start.24
  398.4 1.1 copy-start.23
  399.1 0.8 copy-start.22
  399.4 86.4 %copy-start.21 = (bf16[8,1,32,128]{3,2,1,0:T(8,128)(2,1)S(1)}, bf16[8,1,32,128]{3,2,1,0:T(8,128)(2,1)}, u32[]{:S(2)}) copy-start(bf16[8,1,32,128]{3,2,1,0:T(8,128)(2,1)} %copy-done.20) | copy-start | bytes 196612
  399.4 86.8 %copy-start.19 = (bf16[8,1,32,128]{3,2,1,0:T(8,128)(2,1)S(1)}, bf16[8,1,32,128]{3,2,1,0:T(8,128)(2,1)}, u32[]{:S(2)}) copy-start(bf16[8,1,32,128]{3,2,1,0:T(8,128)(2,1)} %copy-done.18) | copy-start | bytes 196612
  399.5 86.8 %copy-start.29 = (pred[2]{0:T(512)(128)(4,1)S(1)}, pred[2]{0:T(512)(128)(4,1)}, u32[]{:S(2)}) copy-start(pred[2]{0:T(512)(128)(4,1)} %iota_compare_fusion.3) | copy-start | bytes 10
  399.8 86.9 %copy-start.17 = (bf16[8,1,32,128]{3,2,1,0:T(8,128)(2,1)S(1)}, bf16[8,1,32,128]{3,2,1,0:T(8,128)(2,1)}, u32[]{:S(2)}) copy-start(bf16[8,1,32,128]{3,2,1,0:T(8,128)(2,1)} %copy-done.16) | copy-start | bytes 196612
  399.8 86.9 %copy-start.28 = (pred[3]{0:T(512)(128)(4,1)S(1)}, pred[3]{0:T(512)(128)(4,1)}, u32[]{:S(2)}) copy-start(pred[3]{0:T(512)(128)(4,1)} %iota_compare_fusion.2) | copy-start | bytes 13
  399.9 87.3 %copy-start.15 = (bf16[8,1,32,128]{3,2,1,0:T(8,128)(2,1)S(1)}, bf16[8,1,32,128]{3,2,1,0:T(8,128)(2,1)}, u32[]{:S(2)}) copy-start(bf16[8,1,32,128]{3,2,1,0:T(8,128)(2,1)} %copy-done.14) | copy-start | bytes 196612
  399.9 87.3 %copy-start.27 = (pred[4]{0:T(512)(128)(4,1)S(1)}, pred[4]{0:T(512)(128)(4,1)}, u32[]{:S(2)}) copy-start(pred[4]{0:T(512)(128)(4,1)} %iota_compare_fusion.1) | copy-start | bytes 16
  486.5 80.0 %copy-start.13 = (f32[8,8,4]{0,2,1:T(4,128)S(1)}, f32[8,8,4]{0,2,1:T(4,128)}, u32[]{:S(2)}) copy-start(f32[8,8,4]{0,2,1:T(4,128)} %copy.186) | copy-start | bytes 3076
  486.5 80.0 %copy-start.9 = (f32[8,8,4,128]{3,2,1,0:T(4,128)S(1)}, f32[8,8,4,128]{3,2,1,0:T(4,128)}, u32[]{:S(2)}) copy-start(f32[8,8,4,128]{3,2,1,0:T(4,128)} %fusion.26) | copy-start | bytes 393220
  486.7 80.6 %copy-start.8 = (f32[8,8,4,128]{3,2,1,0:T(4,128)S(1)}, f32[8,8,4,128]{3,2,1,0:T(4,128)}, u32[]{:S(2)}) copy-start(f32[8,8,4,128]{3,2,1,0:T(4,128)} %fusion.28) | copy-start | bytes 393220
  487.0 81.1 %copy-start.7 = (f32[8,8,4,128]{3,2,1,0:T(4,128)S(1)}, f32[8,8,4,128]{3,2,1,0:T(4,128)}, u32[]{:S(2)}) copy-start(f32[8,8,4,128]{3,2,1,0:T(4,128)} %fusion.24) | copy-start | bytes 393220
  487.1 81.7 %copy-start.10 = (f32[8,8,4,128]{3,2,1,0:T(4,128)S(1)}, f32[8,8,4,128]{3,2,1,0:T(4,128)}, u32[]{:S(2)}) copy-start(f32[8,8,4,128]{3,2,1,0:T(4,128)} %fusion.22) | copy-start | bytes 393220
Sparse Core Ops, SparseCore 0:
  110.0 286.3 all-reduce.9
  647.2 217.4 all-reduce.11
where the time goes:
time: 886 us; the launch traced here: 875 us
  blocking collectives  519 us (59%)
  waiting for transfers between devices  302 us (34%)
  matrix products  16 us (2%)
  other arithmetic  15.5 us (2%)
  between operations  14.6 us (2%)
    psum x1, waiting for transfers between devices, shards(): lax.psum((factor * cache_total, factor[..., None] * cache_mix), 'tensor')  217 us
    psum x1, blocking collectives, shards(): total_down, total_up = lax.psum((down_gradient, up_gradient), 'dp')  142 us
    psum x1, blocking collectives, shards(): lax.psum((local_projection, local_backward), 'tensor')  94.3 us
    psum x1, blocking collectives, shards(): collected.append(lax.psum(local_kv, 'tensor').astype(jnp.bfloat16))  85.6 us
    psum x1, waiting for transfers between devices, shards(): total_down, total_up = lax.psum((down_gradient, up_gradient), 'dp')  84.9 us
    pmax x1, blocking collectives, shards(): highest = lax.pmax(jnp.maximum(block_high, new_high), 'tensor')  77.3 us
    psum x1, blocking collectives, shards(): lax.psum((factor * cache_total, factor[..., None] * cache_mix), 'tensor')  77.3 us
    all_gather x1, blocking collectives, shards(): lax.all_gather(updated_up.astype(jnp.bfloat16), 'tensor', axis=2, tiled=T...  42.5 us
  transfers between devices with their start and end apart: 2, of which 2 were waited for; matrix products, arithmetic and copies ran while one was open for 2% of the time, Pallas kernels for 0%

commit v1 on v0

v1 whole, which is shorter than its diff:
```python
import functools
import math

import jax
import jax.numpy as jnp
from jax import lax
from jax.experimental import pallas as pl
from jax.experimental.pallas import tpu as pltpu
from jax.sharding import PartitionSpec as P

MESH = pl.DeviceIdType.MESH
F32 = jnp.float32
BF16 = jnp.bfloat16

N_DP = 32
N_TP = 16
RANK = 64
SEQ_DEV = 8
SEQ_LEN = 32
TOK = SEQ_DEV * SEQ_LEN
FEAT = 512
ROWS = 8
STEPS = 4
CACHE_DEV = 48
KVH = 8
HD = 128
KVW = KVH * HD
TILES = 32
UP_TILES = 4
UP_STRIDE = 10

adapter_scale = 2.0
step_size = 0.004
masked_score = -1e30
score_scale = 1.0 / math.sqrt(HD)

(X, COT, DOWN, UP, HID, FRO, QRY, KEY, VAL) = range(9)
(RS1, AG1, RS2, RS2U, AG2, AG2U, BASE, MIX, STAT, LOW, UPX) = range(11)


def dot(a, b):
    return lax.dot_general(a, b, (((1,), (0,)), ((), ())), preferred_element_type=F32)


def dot_nt(a, b):
    return lax.dot_general(a, b, (((1,), (1,)), ((), ())), preferred_element_type=F32)


def iota(shape, axis):
    return lax.broadcasted_iota(jnp.int32, shape, axis)


def kernel(
    rew,
    gid,
    lens,
    x_h,
    cot_h,
    down_h,
    up_h,
    hid_h,
    fro_h,
    q_h,
    k_h,
    v_h,
    od,
    ou,
    oa,
    x,
    cot,
    down,
    up,
    hid,
    fro,
    qry,
    key,
    val,
    hid_f,
    wt,
    pb_send,
    rs1,
    ag1,
    g_send,
    rs2,
    rs2u,
    ag2,
    base_send,
    base_r,
    mix_send,
    mix_r,
    st_send,
    st_r,
    low_send,
    low_r,
    upx_send,
    upx_r,
    qp,
    cmix,
    cmax,
    ctot,
    base_s,
    in_sem,
    send,
    recv,
):
    dp = lax.axis_index("dp")
    tp = lax.axis_index("tensor")

    hbm = (x_h, cot_h, down_h, up_h, hid_h, fro_h, q_h, k_h, v_h)
    vmem = (x, cot, down, up, hid, fro, qry, key, val)
    loads = [pltpu.make_async_copy(h, v, in_sem.at[n]) for n, (h, v) in enumerate(zip(hbm, vmem))]
    for load in loads:
        load.start()

    barrier = pltpu.get_barrier_semaphore()

    def greet_tp(s, c):
        pl.semaphore_signal(
            barrier, inc=1, device_id={"tensor": lax.rem(tp + s, N_TP)}, device_id_type=MESH
        )
        return c

    def greet_dp(s, c):
        pl.semaphore_signal(
            barrier, inc=1, device_id={"dp": lax.rem(dp + s, N_DP)}, device_id_type=MESH
        )
        return c

    lax.fori_loop(1, N_TP, greet_tp, 0)
    lax.fori_loop(1, N_DP, greet_dp, 0)

    def to_tp(src, dst, chan):
        def body(s, c):
            peer = lax.rem(tp + s, N_TP)
            pltpu.make_async_remote_copy(
                src_ref=src(peer),
                dst_ref=dst(s),
                send_sem=send.at[chan],
                recv_sem=recv.at[chan],
                device_id={"tensor": peer},
                device_id_type=MESH,
            ).start()
            return c

        lax.fori_loop(1, N_TP, body, 0)

    def to_dp(src, dst, chan):
        def body(s, c):
            peer = lax.rem(dp + s, N_DP)
            pltpu.make_async_remote_copy(
                src_ref=src(peer),
                dst_ref=dst(s),
                send_sem=send.at[chan],
                recv_sem=recv.at[chan],
                device_id={"dp": peer},
                device_id_type=MESH,
            ).start()
            return c

        lax.fori_loop(1, N_DP, body, 0)

    def landed(ref, chan):
        pltpu.make_async_copy(ref, ref, recv.at[chan]).wait()

    def sent(ref, chan):
        pltpu.make_async_copy(ref, ref, send.at[chan]).wait()

    def summed(own, ref, count):
        return lax.fori_loop(0, count, lambda s, acc: acc + ref[s].astype(F32), own.astype(F32))

    lane_seq = lax.div(iota((1, TOK), 1), SEQ_LEN)
    rew_l = jnp.zeros((1, TOK), F32)
    gid_l = jnp.zeros((1, TOK), jnp.int32)
    for s in range(SEQ_DEV):
        rew_l = jnp.where(lane_seq == s, rew[s], rew_l)
        gid_l = jnp.where(lane_seq == s, gid[s], gid_l)
    cnt = jnp.zeros((1, TOK), F32)
    tot = jnp.zeros((1, TOK), F32)
    for s in range(SEQ_DEV):
        same = gid_l == gid[s]
        cnt = cnt + jnp.where(same, 1.0, 0.0)
        tot = tot + jnp.where(same, rew[s], 0.0)
    mean = tot / cnt
    spread = jnp.zeros((1, TOK), F32)
    for s in range(SEQ_DEV):
        off = rew[s] - mean
        spread = spread + jnp.where(gid_l == gid[s], off * off, 0.0)
    adv = (rew_l - mean) / jnp.maximum(jnp.sqrt(spread / cnt), 1.0)
    token_weight = adv / SEQ_LEN

    loads[X].wait()
    loads[COT].wait()
    loads[DOWN].wait()
    loads[UP].wait()
    proj = dot_nt(down[...].astype(BF16), x[...])
    pb_send[0:8] = proj.astype(BF16).reshape(8, 16, TOK)
    wt[...] = (cot[...].astype(F32) * token_weight).astype(BF16)
    same_k = lax.div(iota((128, 128), 0), RANK) == lax.div(iota((128, 128), 1), RANK)
    up2 = jnp.concatenate([up[...], up[...]], axis=1)
    back = dot(jnp.where(same_k, up2, 0.0).astype(BF16), wt[...])
    pb_send[8:16] = back.astype(BF16).reshape(8, 16, TOK)

    pl.semaphore_wait(barrier, N_TP + N_DP - 2)
    to_tp(lambda peer: pb_send.at[peer], lambda s: rs1.at[s - 1], RS1)

    loads[HID].wait()
    for i in range(ROWS):
        hid_f[STEPS * i : STEPS * (i + 1), :] = hid[i].astype(F32)
    loads[FRO].wait()
    hid_b = hid_f[...].astype(BF16)
    for kv in range(2):
        for part in range(4):
            cols = slice(part * 256, (part + 1) * 256)
            block = dot(hid_b, fro[kv, :, cols]).astype(BF16)
            base_send[2 * part, kv] = block[:, 0:HD]
            base_send[2 * part + 1, kv] = block[:, HD : 2 * HD]

    landed(rs1, RS1)
    ag1[tp] = summed(pb_send[tp], rs1, N_TP - 1).astype(BF16)
    to_tp(lambda peer: ag1.at[tp], lambda s: ag1.at[tp], AG1)
    to_tp(lambda peer: base_send.at[lax.div(peer, 2)], lambda s: base_r.at[s - 1], BASE)

    loads[QRY].wait()
    loads[KEY].wait()
    loads[VAL].wait()
    out_row = iota((128, 128), 0)
    head = 2 * lax.div(out_row, 8) + lax.rem(lax.div(out_row, STEPS), 2)
    source = lax.rem(out_row, STEPS) * 32 + head
    perm = jnp.where(iota((128, 128), 1) == source, 1.0, 0.0).astype(BF16)
    lane_n = iota((128, CACHE_DEV * KVH), 1)
    own_group = lax.rem(lane_n, KVH) == lax.div(iota((128, CACHE_DEV * KVH), 0), 16)
    position = tp * CACHE_DEV + lax.div(lane_n, KVH)
    st_lane = iota((128, 128), 1)

    def attend(i, stats):
        q = dot(perm, qry[i])
        qp[i] = q
        score = dot_nt(q.astype(BF16), key[i]) * score_scale
        valid = jnp.logical_and(own_group, position < lens[i])
        score = jnp.where(valid, score, masked_score)
        high = jnp.max(score, axis=1, keepdims=True)
        weight = jnp.where(valid, jnp.exp(score - high), 0.0)
        total = jnp.sum(weight, axis=1, keepdims=True)
        mix = dot(weight.astype(BF16), val[i])
        stats = jnp.where(st_lane == i, high, stats)
        stats = jnp.where(st_lane == i + ROWS, total, stats)
        return mix.reshape(N_TP, 8, HD), stats

    def attend_pair(n, stats):
        m0, stats = attend(2 * n, stats)
        m1, stats = attend(2 * n + 1, stats)
        mix_send[:, pl.ds(pl.multiple_of(16 * n, 16), 16), :] = jnp.concatenate(
            [m0, m1], axis=1
        ).astype(BF16)
        return stats

    stats = lax.fori_loop(0, 2, attend_pair, jnp.zeros((128, 128), F32))

    landed(ag1.at[pl.ds(0, N_TP - 1)], AG1)
    g_down = dot(ag1[8:16].reshape(128, TOK), x[...]).astype(BF16)
    for n in range(TILES):
        r, c = n // 4, n % 4
        g_send[n] = g_down[16 * r : 16 * (r + 1), 128 * c : 128 * (c + 1)]
    g_up = dot_nt(ag1[0:8].reshape(128, TOK), wt[...])
    first_half = iota((RANK, 128), 1) < RANK
    g_up = jnp.where(first_half, g_up[0:RANK], g_up[RANK:])
    g_send[TILES : TILES + UP_TILES] = g_up.astype(BF16).reshape(UP_TILES, 16, 128)

    to_dp(lambda peer: g_send.at[peer], lambda s: rs2.at[s - 1], RS2)
    up_owner = lax.rem(dp, UP_STRIDE) == 0
    up_tile = TILES + lax.div(dp, UP_STRIDE)
    for u in range(UP_TILES):
        peer = UP_STRIDE * u

        @pl.when(dp != peer)
        def _(u=u, peer=peer):
            pltpu.make_async_remote_copy(
                src_ref=g_send.at[TILES + u],
                dst_ref=rs2u.at[lax.rem(peer - dp + N_DP, N_DP) - 1],
                send_sem=send.at[RS2U],
                recv_sem=recv.at[RS2U],
                device_id={"dp": peer},
                device_id_type=MESH,
            ).start()

    stats = lax.fori_loop(2, 4, attend_pair, stats)
    st_send[...] = stats.reshape(N_TP, 8, 128)
    to_tp(lambda peer: st_send.at[peer], lambda s: st_r.at[s - 1], STAT)
    to_tp(lambda peer: mix_send.at[peer], lambda s: mix_r.at[s - 1], MIX)

    landed(rs2, RS2)
    ag2[dp] = summed(g_send[dp], rs2, N_DP - 1).astype(BF16)
    to_dp(lambda peer: ag2.at[dp], lambda s: ag2.at[dp], AG2)

    @pl.when(up_owner)
    def _():
        landed(rs2u, RS2U)
        ag2[up_tile] = summed(g_send[up_tile], rs2u, N_DP - 1).astype(BF16)
        to_dp(lambda peer: ag2.at[up_tile], lambda s: ag2.at[up_tile], AG2U)

    landed(base_r, BASE)
    base = lax.fori_loop(
        0,
        N_TP - 1,
        lambda s, acc: acc + base_r[s].astype(F32),
        base_send[lax.div(tp, 2)].astype(F32),
    )
    base_s[...] = base
    landed(st_r, STAT)
    landed(mix_r, MIX)
    own_st = st_send[tp]
    top = lax.fori_loop(0, N_TP - 1, lambda s, acc: jnp.maximum(acc, st_r[s]), own_st)

    def part(st, mix, total, acc):
        factor = jnp.exp(st - top)
        total = total + factor * pltpu.roll(st, 128 - ROWS, 1)
        acc = tuple(
            acc[i] + factor[:, i : i + 1] * mix[8 * i : 8 * (i + 1)].astype(F32)
            for i in range(ROWS)
        )
        return total, acc

    zero = jnp.zeros((8, 128), F32)
    carry = part(own_st, mix_send[tp], zero, (zero,) * ROWS)
    total, acc = lax.fori_loop(
        0, N_TP - 1, lambda s, carry: part(st_r[s], mix_r[s], *carry), carry
    )
    for i in range(ROWS):
        rows = slice(8 * i, 8 * (i + 1))
        cmix[rows, :] = acc[i]
        cmax[rows, :] = jnp.broadcast_to(top[:, i : i + 1], (8, 128))
        ctot[rows, :] = jnp.broadcast_to(total[:, i : i + 1], (8, 128))

    landed(ag2.at[pl.ds(0, N_DP - 1)], AG2)
    for n in range(TILES):
        r, c = n // 4, n % 4
        rows, cols = slice(16 * r, 16 * (r + 1)), slice(128 * c, 128 * (c + 1))
        od[rows, cols] = down[rows, cols] + step_size * (adapter_scale * ag2[n].astype(F32))
    low = dot_nt(hid_b, od[...].astype(BF16))
    low_send[...] = low.astype(BF16)
    to_tp(lambda peer: low_send, lambda s: low_r.at[s - 1], LOW)

    @pl.when(up_owner)
    def _():
        landed(ag2.at[pl.ds(0, UP_TILES - 1)], AG2U)

    @pl.when(jnp.logical_not(up_owner))
    def _():
        landed(ag2.at[pl.ds(0, UP_TILES)], AG2U)

    up_old = jnp.where(first_half, up2[0:RANK], up2[RANK:])
    up_grad = ag2[TILES : TILES + UP_TILES].reshape(RANK, 128).astype(F32)
    up_new = up_old + step_size * (adapter_scale * up_grad)
    ou[0:RANK] = up_new[:, 0:RANK]
    ou[RANK:] = pltpu.roll(up_new, RANK, 1)[:, 0:RANK]
    upx_send[...] = up_new.astype(BF16)
    pair = tp + 1 - 2 * lax.rem(tp, 2)
    swap = pltpu.make_async_remote_copy(
        src_ref=upx_send,
        dst_ref=upx_r,
        send_sem=send.at[UPX],
        recv_sem=recv.at[UPX],
        device_id={"tensor": pair},
        device_id_type=MESH,
    )
    swap.start()

    own_q = qp[:, pl.ds(pl.multiple_of(8 * tp, 8), 8), :].reshape(64, HD).astype(BF16)

    swap.wait_recv()
    even = lax.rem(tp, 2) == 0
    mine = upx_send[...].astype(F32)
    theirs = upx_r[...].astype(F32)
    left = jnp.where(even, mine, theirs)
    right = jnp.where(even, theirs, mine)
    up_k = jnp.where(first_half, left, pltpu.roll(right, RANK, 1)).astype(BF16)
    up_v = jnp.where(first_half, pltpu.roll(left, RANK, 1), right).astype(BF16)

    landed(low_r, LOW)
    low = summed(low_send[...], low_r, N_TP - 1).astype(BF16)
    new_k = (base_s[0] + adapter_scale * dot(low[:, 0:RANK], up_k)).astype(BF16)
    new_v = (base_s[1] + adapter_scale * dot(low[:, RANK:], up_v)).astype(BF16)
    row = iota((64, 32), 0)
    col = iota((64, 32), 1)
    causal = jnp.logical_and(
        lax.div(row, 8) == lax.div(col, STEPS), lax.rem(col, STEPS) <= lax.rem(row, STEPS)
    )
    score = jnp.where(causal, dot_nt(own_q, new_k) * score_scale, masked_score)
    new_high = jnp.max(score, axis=1, keepdims=True)
    weight = jnp.where(causal, jnp.exp(score - new_high), 0.0)
    new_total = jnp.sum(weight, axis=1, keepdims=True)
    new_mix = dot(weight.astype(BF16), new_v)
    old_high = cmax[...]
    highest = jnp.maximum(old_high, new_high)
    f_old = jnp.exp(old_high - highest)
    f_new = jnp.exp(new_high - highest)
    out = (f_old * cmix[...] + f_new * new_mix) / (f_old * ctot[...] + f_new * new_total)
    out = out.reshape(ROWS, 8, HD)
    oa[:, :, 0:HD] = out[:, 0:STEPS].astype(BF16)
    oa[:, :, HD:] = out[:, STEPS:].astype(BF16)

    sent(rs1, RS1)
    sent(rs1, AG1)
    sent(base_r, BASE)
    sent(st_r, STAT)
    sent(mix_r, MIX)
    sent(rs2, RS2)
    sent(rs2, AG2)
    sent(low_r, LOW)
    swap.wait_send()

    @pl.when(up_owner)
    def _():
        sent(ag2.at[pl.ds(0, UP_TILES - 1)], RS2U)
        sent(rs2u, AG2U)

    @pl.when(jnp.logical_not(up_owner))
    def _():
        sent(ag2.at[pl.ds(0, UP_TILES)], RS2U)


def shards(
    learn_input,
    cotangent,
    rewards,
    group_ids,
    adapter_down,
    adapter_up,
    frozen_weight,
    hidden,
    queries,
    key_cache,
    value_cache,
    cache_lengths,
):
    smem = pl.BlockSpec(memory_space=pltpu.SMEM)
    hbm = pl.BlockSpec(memory_space=pl.ANY)
    vmem = pl.BlockSpec(memory_space=pltpu.VMEM)
    operands = (
        learn_input,
        jnp.transpose(cotangent, (1, 2, 0)).reshape(128, TOK),
        adapter_down.reshape(128, FEAT),
        adapter_up.reshape(128, RANK),
        hidden,
        frozen_weight,
        queries.reshape(ROWS, 128, HD),
        key_cache.reshape(ROWS, CACHE_DEV * KVH, HD),
        value_cache.reshape(ROWS, CACHE_DEV * KVH, HD),
    )
    out_down, out_up, attended = pl.pallas_call(
        kernel,
        out_shape=(
            jax.ShapeDtypeStruct((128, FEAT), F32),
            jax.ShapeDtypeStruct((128, RANK), F32),
            jax.ShapeDtypeStruct((ROWS, STEPS, 2 * HD), BF16),
        ),
        in_specs=[smem] * 3 + [hbm] * 9,
        out_specs=(vmem, vmem, vmem),
        scratch_shapes=[pltpu.VMEM(o.shape, o.dtype) for o in operands]
        + [
            pltpu.VMEM((ROWS * STEPS, FEAT), F32),
            pltpu.VMEM((128, TOK), BF16),
            pltpu.VMEM((16, 16, TOK), BF16),
            pltpu.VMEM((15, 16, TOK), BF16),
            pltpu.VMEM((16, 16, TOK), BF16),
            pltpu.VMEM((36, 16, 128), BF16),
            pltpu.VMEM((31, 16, 128), BF16),
            pltpu.VMEM((31, 16, 128), BF16),
            pltpu.VMEM((36, 16, 128), BF16),
            pltpu.VMEM((8, 2, 32, HD), BF16),
            pltpu.VMEM((15, 2, 32, HD), BF16),
            pltpu.VMEM((16, 64, HD), BF16),
            pltpu.VMEM((15, 64, HD), BF16),
            pltpu.VMEM((16, 8, 128), F32),
            pltpu.VMEM((15, 8, 128), F32),
            pltpu.VMEM((32, 128), BF16),
            pltpu.VMEM((15, 32, 128), BF16),
            pltpu.VMEM((RANK, 128), BF16),
            pltpu.VMEM((RANK, 128), BF16),
            pltpu.VMEM((ROWS, 128, HD), F32),
            pltpu.VMEM((64, HD), F32),
            pltpu.VMEM((64, HD), F32),
            pltpu.VMEM((64, HD), F32),
            pltpu.VMEM((2, 32, HD), F32),
            pltpu.SemaphoreType.DMA((9,)),
            pltpu.SemaphoreType.DMA((11,)),
            pltpu.SemaphoreType.DMA((11,)),
        ],
        compiler_params=pltpu.CompilerParams(
            collective_id=0, has_side_effects=True, vmem_limit_bytes=32 * 1024 * 1024
        ),
    )(rewards, group_ids, cache_lengths, *operands)
    return (
        out_down.reshape(2, RANK, FEAT),
        out_up.reshape(2, RANK, RANK),
        attended,
    )


def solution(mesh):
    return jax.shard_map(
        shards,
        mesh=mesh,
        in_specs=(
            P("dp", "tensor"),
            P("dp", None, "tensor"),
            P("dp"),
            P("dp"),
            P(None, None, "tensor"),
            P(None, None, "tensor"),
            P(None, "tensor", None),
            P("dp", None, "tensor"),
            P("dp", None, None, None),
            P("dp", "tensor", None, None),
            P("dp", "tensor", None, None),
            P("dp"),
        ),
        out_specs=(P(None, None, "tensor"), P(None, None, "tensor"), P("dp", None, "tensor")),
        check_vma=False,
    )
```

time: 886 us -> 75.8 us (0.09); the launches traced: 875 us -> 75.3 us
  blocking collectives: 519 us -> 0 us
  waiting for transfers between devices: 302 us -> 0 us
  Pallas kernels: 0 us -> 61.6 us
  matrix products: 16 us -> 0 us
  other arithmetic: 15.5 us -> 0 us
  between operations: 14.6 us -> 0.66 us
    psum x4 -> x0, blocking collectives: 399 us -> none  [the longest x1 142 us: shards(): total_down, total_up = lax.psum((down_gradient, up_gradient), 'dp')]
    psum x2 -> x0, waiting for transfers between devices: 302 us -> none  [the longest x1 217 us: shards(): lax.psum((factor * cache_total, factor[..., None] * cache_mix), 'tensor')]
    pmax x1 -> x0, blocking collectives: 77.3 us -> none  [shards(): highest = lax.pmax(jnp.maximum(block_high, new_high), 'tensor')]
    pallas_call x0 -> x1, Pallas kernels: none -> 61.6 us  [shards(): pl.pallas_call(kernel, out_shape=(jax.ShapeDtypeStruct((128, FEAT), F32),...]
    all_gather x1 -> x0, blocking collectives: 42.5 us -> none  [shards(): lax.all_gather(updated_up.astype(jnp.bfloat16), 'tensor', axis=2, tiled=T...]
    dot_general x24 -> x0, matrix products: 16 us -> none  [the longest x4 5.06 us: shards(): jnp.einsum('rtgqp,rpgd->rtgqd', cache_weight.astype(jnp.bfloat16), value_...]
    unnamed x65 -> x27, local copies, waits for them, and re-layouts: 1.07 us -> 13 us
  transfers between devices with their start and end apart: 2 -> 0, of which waited for: 2 -> 0; matrix products, arithmetic and copies ran while one was open for 2% -> 0% of each run, Pallas kernels for 0% -> 0%
where the time goes in v1:
time: 75.8 us; the launch traced here: 75.3 us
  Pallas kernels  61.6 us (81%)
  local copies, waits for them, and re-layouts  13 us (17%)
    pallas_call x1, Pallas kernels, shards(): pl.pallas_call(kernel, out_shape=(jax.ShapeDtypeStruct((128, FEAT), F32),...  61.6 us
    unnamed x27, local copies, waits for them, and re-layouts  13 us

profile of v1, /device:TPU:1, one launch (start us, length us, event | category | flops | bytes accessed | tf_op | source)
XLA Modules:
  0.0 75.3 jit_solution(11581303342862006757)
XLA Ops:
  0.6 0.0 copy-start
  0.6 1.6 %copy-done = bf16[2,512,1024]{2,1,0:T(8,128)(2,1)S(1)} copy-done((bf16[2,512,1024]{2,1,0:T(8,128)(2,1)S(1)}, bf16[2,512,1024]{2,1,0:T(8,128)(2,1)}, u32[]{:S(2)}) %copy-start) | copy-done | bytes 2097176
  2.2 0.0 copy-start.1
  2.2 1.1 %copy-done.1 = bf16[8,48,8,128]{3,2,1,0:T(8,128)(2,1)S(1)} copy-done((bf16[8,48,8,128]{3,2,1,0:T(8,128)(2,1)S(1)}, bf16[8,48,8,128]{3,2,1,0:T(8,128)(2,1)}, u32[]{:S(2)}) %copy-start.1) | copy-done | bytes 786456
  3.4 0.0 copy-start.2
  3.4 1.1 %copy-done.2 = bf16[8,48,8,128]{3,2,1,0:T(8,128)(2,1)S(1)} copy-done((bf16[8,48,8,128]{3,2,1,0:T(8,128)(2,1)S(1)}, bf16[8,48,8,128]{3,2,1,0:T(8,128)(2,1)}, u32[]{:S(2)}) %copy-start.2) | copy-done | bytes 786456
  4.5 0.0 copy-start.3
  4.5 0.9 %copy-done.3 = bf16[256,512]{1,0:T(8,128)(2,1)S(1)} copy-done((bf16[256,512]{1,0:T(8,128)(2,1)S(1)}, bf16[256,512]{1,0:T(8,128)(2,1)}, u32[]{:S(2)}) %copy-start.3) | copy-done | bytes 262168
  5.4 0.0 copy-start.4
  5.4 0.9 %copy-done.4 = f32[2,64,512]{2,1,0:T(8,128)S(1)} copy-done((f32[2,64,512]{2,1,0:T(8,128)S(1)}, f32[2,64,512]{2,1,0:T(8,128)}, u32[]{:S(2)}) %copy-start.4) | copy-done | bytes 262168
  6.4 0.0 copy-start.5
  6.4 0.9 %copy-done.5 = bf16[8,4,32,128]{3,2,1,0:T(8,128)(2,1)S(1)} copy-done((bf16[8,4,32,128]{3,2,1,0:T(8,128)(2,1)S(1)}, bf16[8,4,32,128]{3,2,1,0:T(8,128)(2,1)}, u32[]{:S(2)}) %copy-start.5) | copy-done | bytes 262168
  7.3 0.0 copy-start.6
  7.3 0.8 %copy-done.6 = bf16[256,2,64]{0,2,1:T(8,128)(2,1)S(1)} copy-done((bf16[256,2,64]{0,2,1:T(8,128)(2,1)S(1)}, bf16[256,2,64]{0,2,1:T(8,128)(2,1)}, u32[]{:S(2)}) %copy-start.6) | copy-done | bytes 65560
  8.2 0.0 copy-start.7
  8.2 0.8 %copy-done.7 = f32[2,64,64]{2,1,0:T(8,128)S(1)} copy-done((f32[2,64,64]{2,1,0:T(8,128)S(1)}, f32[2,64,64]{2,1,0:T(8,128)}, u32[]{:S(2)}) %copy-start.7) | copy-done | bytes 32792
  9.0 0.0 copy-start.8
  9.0 0.8 %copy-done.8 = bf16[8,4,512]{2,1,0:T(4,128)(2,1)S(1)} copy-done((bf16[8,4,512]{2,1,0:T(4,128)(2,1)S(1)}, bf16[8,4,512]{2,1,0:T(4,128)(2,1)}, u32[]{:S(2)}) %copy-start.8) | copy-done | bytes 32792
  9.8 0.0 copy-start.9
  9.8 0.7 copy-done.9
  10.4 0.0 copy-start.10
  10.4 0.7 copy-done.10
  11.1 0.0 copy-start.11
  11.1 0.7 copy-done.11
  11.8 61.6 %shard_map.139 = (f32[128,512]{1,0:T(8,128)S(1)}, f32[128,64]{1,0:T(8,128)S(1)}, bf16[8,4,256]{2,1,0:T(4,128)(2,1)S(1)}) custom-call(f32[8]{0:T(128)S(1)} %copy-done.9, s32[8]{0:T(128)S(1)} %copy-done.10, s32[8]{0:T(128)S(1)} %copy-done.11, bf16[256,512]{1,0:T(8,128)(2,1)S(1)} %copy-done.3, bf16[128,256]{1,0:T(8,128)(2,1)S(1)} %bitcast.15, ...), custom_call_target="tpu_custom_call" | custom-call | tf_op jit(solution)/shard_map/pallas_call | solution.py:450
  73.3 0.7 copy.18
  74.0 0.6 copy.19
  74.7 0.6 copy.20
Async XLA Ops:
  0.6 1.6 %copy-start = (bf16[2,512,1024]{2,1,0:T(8,128)(2,1)S(1)}, bf16[2,512,1024]{2,1,0:T(8,128)(2,1)}, u32[]{:S(2)}) copy-start(bf16[2,512,1024]{2,1,0:T(8,128)(2,1)} %fro_h.1) | copy-start | bytes 6291460
  2.2 1.1 %copy-start.1 = (bf16[8,48,8,128]{3,2,1,0:T(8,128)(2,1)S(1)}, bf16[8,48,8,128]{3,2,1,0:T(8,128)(2,1)}, u32[]{:S(2)}) copy-start(bf16[8,48,8,128]{3,2,1,0:T(8,128)(2,1)} %param.21) | copy-start | bytes 2359300
  3.4 1.1 %copy-start.2 = (bf16[8,48,8,128]{3,2,1,0:T(8,128)(2,1)S(1)}, bf16[8,48,8,128]{3,2,1,0:T(8,128)(2,1)}, u32[]{:S(2)}) copy-start(bf16[8,48,8,128]{3,2,1,0:T(8,128)(2,1)} %param.22) | copy-start | bytes 2359300
  4.5 0.9 %copy-start.3 = (bf16[256,512]{1,0:T(8,128)(2,1)S(1)}, bf16[256,512]{1,0:T(8,128)(2,1)}, u32[]{:S(2)}) copy-start(bf16[256,512]{1,0:T(8,128)(2,1)} %x_h.1) | copy-start | bytes 786436
  5.4 0.9 %copy-start.4 = (f32[2,64,512]{2,1,0:T(8,128)S(1)}, f32[2,64,512]{2,1,0:T(8,128)}, u32[]{:S(2)}) copy-start(f32[2,64,512]{2,1,0:T(8,128)} %param.16) | copy-start | bytes 786436
  6.4 0.9 %copy-start.5 = (bf16[8,4,32,128]{3,2,1,0:T(8,128)(2,1)S(1)}, bf16[8,4,32,128]{3,2,1,0:T(8,128)(2,1)}, u32[]{:S(2)}) copy-start(bf16[8,4,32,128]{3,2,1,0:T(8,128)(2,1)} %param.20) | copy-start | bytes 786436
  7.3 0.8 %copy-start.6 = (bf16[256,2,64]{0,2,1:T(8,128)(2,1)S(1)}, bf16[256,2,64]{0,2,1:T(8,128)(2,1)}, u32[]{:S(2)}) copy-start(bf16[256,2,64]{0,2,1:T(8,128)(2,1)} %param.13) | copy-start | bytes 196612
  8.2 0.8 %copy-start.7 = (f32[2,64,64]{2,1,0:T(8,128)S(1)}, f32[2,64,64]{2,1,0:T(8,128)}, u32[]{:S(2)}) copy-start(f32[2,64,64]{2,1,0:T(8,128)} %param.17) | copy-start | bytes 98308
  9.0 0.8 %copy-start.8 = (bf16[8,4,512]{2,1,0:T(4,128)(2,1)S(1)}, bf16[8,4,512]{2,1,0:T(4,128)(2,1)}, u32[]{:S(2)}) copy-start(bf16[8,4,512]{2,1,0:T(4,128)(2,1)} %hid_h.1) | copy-start | bytes 98308
  9.8 0.7 copy-start.9
  10.4 0.7 copy-start.10
  11.1 0.7 copy-start.11

commit v2 on v1

v2 whole, which is shorter than its diff:
```python
import math

import jax
import jax.numpy as jnp
from jax import lax
from jax.experimental import pallas as pl
from jax.experimental.pallas import tpu as pltpu
from jax.sharding import PartitionSpec as P

MESH = pl.DeviceIdType.MESH
F32 = jnp.float32
BF16 = jnp.bfloat16

N_TP = 16
N_Y = 8
N_CHIP = 16
RANK = 64
SEQ_DEV = 8
SEQ_LEN = 32
TOK = SEQ_DEV * SEQ_LEN
FEAT = 512
ROWS = 8
STEPS = 4
CACHE_DEV = 48
KVH = 8
HD = 128
UP_OWNERS = (5, 10)
VMEM_LIMIT = 60 * 1024 * 1024

adapter_scale = 2.0
step_size = 0.004
masked_score = -1e30
score_scale = 1.0 / math.sqrt(HD)

(REW, GID, COT, UP, X, DOWN, HID, FRO, LEN, QRY, KEY, VAL) = range(12)
(
    RS1B,
    RS1P,
    AG1B,
    AG1P,
    XC,
    WC,
    HC,
    RS2,
    RS2U,
    AG2,
    AG2U,
    BASEY,
    BASEZ,
    BASEP,
    MIXY,
    STATY,
    MIXZ,
    STATZ,
    LOW,
    DOWNC,
    UPC,
    UPX,
    N_CHAN,
) = range(23)


def dot(a, b):
    return lax.dot_general(a, b, (((1,), (0,)), ((), ())), preferred_element_type=F32)


def dot_nt(a, b):
    return lax.dot_general(a, b, (((1,), (1,)), ((), ())), preferred_element_type=F32)


def iota(shape, axis):
    return lax.broadcasted_iota(jnp.int32, shape, axis)


def fold(a):
    n = a.shape[0] // 2
    return jnp.concatenate([a[:n], a[n:]], axis=1)


def unfold(a):
    return jnp.concatenate([a[:, :RANK], a[:, RANK:]], axis=0)


def by_tiles(tiles):
    return jnp.concatenate(
        [jnp.concatenate([tiles[r, 0], tiles[r, 1]], axis=1) for r in range(4)], axis=0
    )


def kernel(
    rew_h,
    gid_h,
    len_h,
    x_h,
    cot_h,
    down_h,
    up_h,
    hid_h,
    fro_h,
    q_h,
    k_h,
    v_h,
    od_h,
    ou_h,
    oa_h,
    rew,
    gid,
    lens,
    x,
    cot,
    down,
    up,
    hid,
    fro,
    qry,
    key,
    val,
    od,
    ou,
    oa,
    x_c,
    wt,
    wt_c,
    hid_c,
    hid_f,
    pb_send,
    rs1,
    ag1_send,
    ag1,
    g_send,
    rs2,
    ag2,
    ag2_c,
    gu_send,
    rs2u,
    agu,
    agu_c,
    base_send,
    base_r,
    basez_send,
    basez_r,
    basep_send,
    basep_r,
    mix_send,
    mix_r,
    mixz_send,
    mixz_r,
    st_send,
    st_r,
    stz_send,
    stz_r,
    low_send,
    low_r,
    upx_send,
    upx_r,
    qp,
    in_sem,
    out_sem,
    send,
    recv,
):
    dp = lax.axis_index("dp")
    tp = lax.axis_index("tensor")
    chip = lax.div(dp, 2)
    core = lax.rem(dp, 2)
    z_hi = lax.div(tp, N_Y)
    y = lax.rem(tp, N_Y)
    middle = 2 * (chip + 2 - 4 * lax.rem(lax.div(chip, 2), 2))
    other_core = 2 * chip + 1 - core
    pair = tp + 1 - 2 * lax.rem(tp, 2)
    other_half = y + N_Y * (1 - z_hi)

    barrier = pltpu.get_barrier_semaphore()

    def greet(device):
        pl.semaphore_signal(barrier, inc=1, device_id=device, device_id_type=MESH)

    def greet_middle(s, c):
        t = lax.rem(tp + s, N_TP)
        greet({"dp": middle + core, "tensor": t})
        greet({"dp": middle + 1 - core, "tensor": t})
        return c

    def greet_chips(s, c):
        greet({"dp": 2 * lax.rem(chip + s, N_CHIP) + core})
        return c

    lax.fori_loop(0, N_TP, greet_middle, 0)
    lax.fori_loop(1, N_CHIP, greet_chips, 0)
    greet({"dp": other_core})

    hbm = (rew_h, gid_h, cot_h, up_h, x_h, down_h, hid_h, fro_h, len_h, q_h, k_h, v_h)
    own = (rew, gid, cot, up, x, down, hid, fro, lens, qry, key, val)
    loads = [pltpu.make_async_copy(h, v, in_sem.at[n]) for n, (h, v) in enumerate(zip(hbm, own))]
    for load in loads:
        load.start()

    def remote(src, dst, chan, device):
        return pltpu.make_async_remote_copy(
            src_ref=src,
            dst_ref=dst,
            send_sem=send.at[chan],
            recv_sem=recv.at[chan],
            device_id=device,
            device_id_type=MESH,
        )

    def each(first, last, step):
        def body(s, c):
            step(s)
            return c

        lax.fori_loop(first, last, body, 0)

    def landed(ref, chan):
        pltpu.make_async_copy(ref, ref, recv.at[chan]).wait()

    def sent(ref, chan):
        pltpu.make_async_copy(ref, ref, send.at[chan]).wait()

    def summed(first, ref, start, stop):
        return lax.fori_loop(start, stop, lambda s, acc: acc + ref[s].astype(F32), first)

    loads[REW].wait()
    loads[GID].wait()
    lane_seq = lax.div(iota((1, TOK), 1), SEQ_LEN)
    rew_l = jnp.zeros((1, TOK), F32)
    gid_l = jnp.zeros((1, TOK), jnp.int32)
    for s in range(SEQ_DEV):
        rew_l = jnp.where(lane_seq == s, rew[s], rew_l)
        gid_l = jnp.where(lane_seq == s, gid[s], gid_l)
    cnt = jnp.zeros((1, TOK), F32)
    tot = jnp.zeros((1, TOK), F32)
    for s in range(SEQ_DEV):
        same = gid_l == gid[s]
        cnt = cnt + jnp.where(same, 1.0, 0.0)
        tot = tot + jnp.where(same, rew[s], 0.0)
    mean = tot / cnt
    spread = jnp.zeros((1, TOK), F32)
    for s in range(SEQ_DEV):
        off = rew[s] - mean
        spread = spread + jnp.where(gid_l == gid[s], off * off, 0.0)
    adv = (rew_l - mean) / jnp.maximum(jnp.sqrt(spread / cnt), 1.0)
    token_weight = adv / SEQ_LEN

    def put_pieces(part, k, product):
        product = product.astype(BF16)
        for r in range(4):
            for half in range(2):
                pb_send[part, (4 * k + r) * 2 + half] = product[
                    16 * r : 16 * (r + 1), 128 * half : 128 * (half + 1)
                ]

    loads[COT].wait()
    loads[UP].wait()
    for k in range(2):
        wt[k] = (cot[RANK * k : RANK * (k + 1)].astype(F32) * token_weight).astype(BF16)
        put_pieces(0, k, dot(up[k].astype(BF16), wt[k]))
    loads[X].wait()
    loads[DOWN].wait()
    for k in range(2):
        put_pieces(1, k, dot_nt(down[k].astype(BF16), x[...]))
    loads[HID].wait()

    pl.semaphore_wait(barrier, 2 * N_TP + N_CHIP)

    for part, chan in ((0, RS1B), (1, RS1P)):

        def send_piece(s, part=part, chan=chan):
            t = lax.rem(tp + s, N_TP)
            device = {"dp": middle + core, "tensor": t}
            remote(pb_send.at[part, t], rs1.at[part, s], chan, device).start()

        each(0, N_TP, send_piece)
    to_core = {"dp": other_core}
    remote(wt.at[1 - core], wt_c, WC, to_core).start()
    remote(x, x_c, XC, to_core).start()
    remote(hid, hid_c, HC, to_core).start()

    for i in range(ROWS):
        hid_f[STEPS * i : STEPS * (i + 1), :] = hid[i].astype(F32)
    hid_b = hid_f[...].astype(BF16)
    loads[FRO].wait()
    for part in range(4):
        cols = slice(part * 256, (part + 1) * 256)
        new_k = dot(hid_b, fro[0, :, cols]).astype(BF16)
        new_v = dot(hid_b, fro[1, :, cols]).astype(BF16)
        for n in range(4):
            half = slice(RANK * n, RANK * (n + 1))
            base_send[4 * part + n] = jnp.concatenate([new_k[:, half], new_v[:, half]], axis=1)

    loads[LEN].wait()
    loads[QRY].wait()
    loads[KEY].wait()
    loads[VAL].wait()
    out_row = iota((128, 128), 0)
    head = 2 * lax.div(out_row, 8) + lax.rem(lax.div(out_row, STEPS), 2)
    source = lax.rem(out_row, STEPS) * 32 + head
    perm = jnp.where(iota((128, 128), 1) == source, 1.0, 0.0).astype(BF16)
    lane_n = iota((128, CACHE_DEV * KVH), 1)
    own_group = lax.rem(lane_n, KVH) == lax.div(iota((128, CACHE_DEV * KVH), 0), 16)
    position = tp * CACHE_DEV + lax.div(lane_n, KVH)
    st_lane = iota((128, 128), 1)

    def attend(i, stats):
        q = dot(perm, qry[i])
        qp[i] = q
        score = dot_nt(q.astype(BF16), key[i]) * score_scale
        valid = jnp.logical_and(own_group, position < lens[i])
        score = jnp.where(valid, score, masked_score)
        high = jnp.max(score, axis=1, keepdims=True)
        weight = jnp.where(valid, jnp.exp(score - high), 0.0)
        total = jnp.sum(weight, axis=1, keepdims=True)
        mix = dot(weight.astype(BF16), val[i])
        stats = jnp.where(st_lane == i, high, stats)
        stats = jnp.where(st_lane == i + ROWS, total, stats)
        return mix.reshape(N_TP, 8, HD), stats

    def attend_pair(n, stats):
        m0, stats = attend(2 * n, stats)
        m1, stats = attend(2 * n + 1, stats)
        mix_send[:, pl.ds(pl.multiple_of(16 * n, 16), 16), :] = jnp.concatenate(
            [m0, m1], axis=1
        ).astype(BF16)
        return stats

    stats = lax.fori_loop(0, 4, attend_pair, jnp.zeros((128, 128), F32))
    st_send[...] = stats.reshape(N_TP, 8, 128)

    owned_k = lax.div(tp, N_Y)
    owned_r = lax.div(lax.rem(tp, N_Y), 2)
    owned_half = lax.rem(tp, 2)
    for part, chan_in, chan_out in ((0, RS1B, AG1B), (1, RS1P, AG1P)):
        landed(rs1.at[part], chan_in)
        ag1_send[part] = summed(jnp.zeros((16, 128), F32), rs1.at[part], 0, N_TP).astype(BF16)

        def send_sum(s, part=part, chan=chan_out):
            device = {"dp": middle + owned_k, "tensor": lax.rem(tp + s, N_TP)}
            remote(
                ag1_send.at[part], ag1.at[part, core, owned_r, owned_half], chan, device
            ).start()

        each(0, N_TP, send_sum)

    landed(x_c, XC)
    landed(wt_c, WC)
    landed(hid_c, HC)

    landed(ag1.at[0], AG1B)

    g_down = dot(by_tiles(ag1[0, core]), x[...]) + dot(by_tiles(ag1[0, 1 - core]), x_c[...])
    g_down = g_down.astype(BF16)
    for n in range(N_CHIP):
        r, c = n // 4, n % 4
        g_send[n] = g_down[16 * r : 16 * (r + 1), 128 * c : 128 * (c + 1)]

    def send_tile(s):
        q = lax.rem(chip + s, N_CHIP)
        remote(g_send.at[q], rs2.at[s - 1], RS2, {"dp": 2 * q + core}).start()

    each(1, N_CHIP, send_tile)

    landed(ag1.at[1], AG1P)

    g_up = dot_nt(by_tiles(ag1[1, core]), wt[core]) + dot_nt(by_tiles(ag1[1, 1 - core]), wt_c[...])
    gu_send[...] = fold(g_up).astype(BF16).reshape(2, 16, 128)
    for u, q in enumerate(UP_OWNERS):

        @pl.when(chip != q)
        def _(u=u, q=q):
            slot = lax.rem(q - chip + N_CHIP, N_CHIP) - 1
            remote(gu_send.at[u], rs2u.at[slot], RS2U, {"dp": 2 * q + core}).start()

    def send_along_y(s):
        to = lax.rem(y + s, N_Y)
        device = {"tensor": N_Y * z_hi + to}
        for z in range(2):
            t = N_Y * z + to
            remote(base_send.at[t], base_r.at[s - 1, z], BASEY, device).start()

    def send_mix_along_y(s):
        to = lax.rem(y + s, N_Y)
        device = {"tensor": N_Y * z_hi + to}
        for z in range(2):
            t = N_Y * z + to
            remote(st_send.at[t], st_r.at[s - 1, z], STATY, device).start()
            remote(mix_send.at[t], mix_r.at[s - 1, z], MIXY, device).start()

    each(1, N_Y, send_along_y)
    each(1, N_Y, send_mix_along_y)
    for i in range(ROWS):
        hid_f[STEPS * i : STEPS * (i + 1), :] = hid_c[i].astype(F32)
    hid_cb = hid_f[...].astype(BF16)

    landed(rs2, RS2)

    ag2[chip] = summed(g_send[chip].astype(F32), rs2, 0, N_CHIP - 1).astype(BF16)

    def send_total(s):
        q = lax.rem(chip + s, N_CHIP)
        remote(ag2.at[chip], ag2.at[chip], AG2, {"dp": 2 * q + core}).start()

    each(1, N_CHIP, send_total)

    is_owner = jnp.logical_or(chip == UP_OWNERS[0], chip == UP_OWNERS[1])
    up_tile = jnp.where(chip == UP_OWNERS[0], 0, 1)

    @pl.when(is_owner)
    def _():
        landed(rs2u, RS2U)
        agu[up_tile] = summed(gu_send[up_tile].astype(F32), rs2u, 0, N_CHIP - 1).astype(BF16)

        def send_up(s):
            q = lax.rem(chip + s, N_CHIP)
            remote(agu.at[up_tile], agu.at[up_tile], AG2U, {"dp": 2 * q + core}).start()

        each(1, N_CHIP, send_up)

    landed(base_r, BASEY)

    def base_sum(z):
        first = base_send[N_Y * z + y].astype(F32)
        return lax.fori_loop(
            0, N_Y - 1, lambda s, acc: acc + base_r[s, z].astype(F32), first
        )

    to_half = {"tensor": other_half}
    basez_send[...] = base_sum(1 - z_hi)
    remote(basez_send, basez_r, BASEZ, to_half).start()
    base = base_sum(z_hi)

    landed(ag2.at[pl.ds(0, N_CHIP - 1)], AG2)

    def tiles_of(ref):
        return jnp.concatenate(
            [jnp.concatenate([ref[4 * r + c] for c in range(4)], axis=1) for r in range(4)], axis=0
        ).astype(F32)

    new_down = down[core] + step_size * (adapter_scale * tiles_of(ag2))
    roll_down = new_down.astype(BF16)
    low_send[0] = fold(dot_nt(hid_b, roll_down)).astype(BF16)
    low_send[1] = fold(dot_nt(hid_cb, roll_down)).astype(BF16)

    def send_low(s):
        t = lax.rem(tp + s, N_TP)
        remote(low_send.at[0], low_r.at[s], LOW, {"tensor": t}).start()
        remote(
            low_send.at[1], low_r.at[N_TP + s], LOW, {"dp": other_core, "tensor": t}
        ).start()

    each(1, N_TP, send_low)
    remote(low_send.at[1], low_r.at[N_TP], LOW, to_core).start()
    remote(ag2, ag2_c, DOWNC, to_core).start()
    od[core] = new_down

    @pl.when(is_owner)
    def _():
        landed(agu.at[0], AG2U)

    @pl.when(jnp.logical_not(is_owner))
    def _():
        landed(agu, AG2U)

    def up_updated(k, grad):
        return up[k] + step_size * (adapter_scale * unfold(grad.reshape(32, 128)).astype(F32))

    new_up = up_updated(core, agu[...])
    upx_send[...] = fold(new_up).astype(BF16).reshape(2, 16, 128)
    remote(agu, agu_c, UPC, to_core).start()
    remote(upx_send, upx_r.at[0], UPX, {"tensor": pair}).start()
    remote(upx_send, upx_r.at[1], UPX, {"dp": other_core, "tensor": pair}).start()
    ou[core] = new_up

    landed(basez_r, BASEZ)
    base = base + basez_r[...]
    basep_send[...] = base
    remote(basep_send, basep_r, BASEP, {"tensor": pair}).start()

    landed(st_r, STATY)
    landed(mix_r, MIXY)

    def combine(st, mix, count):
        top = st(0)
        for s in range(1, count):
            top = jnp.maximum(top, st(s))
        total = jnp.zeros((8, 128), F32)
        acc = [jnp.zeros((8, 128), F32)] * ROWS
        for s in range(count):
            factor = jnp.exp(st(s) - top)
            total = total + factor * pltpu.roll(st(s), 128 - ROWS, 1)
            block = mix(s)
            for i in range(ROWS):
                acc[i] = acc[i] + factor[:, i : i + 1] * block[8 * i : 8 * (i + 1)].astype(F32)
        return top, total, acc

    def combine_y(z):
        t = N_Y * z + y
        return combine(
            lambda s: st_send[t] if s == 0 else st_r[s - 1, z],
            lambda s: mix_send[t] if s == 0 else mix_r[s - 1, z],
            N_Y,
        )

    def packed(top, total):
        return jnp.where(iota((8, 128), 1) < ROWS, top, pltpu.roll(total, ROWS, 1))

    top, total, acc = combine_y(1 - z_hi)
    stz_send[...] = packed(top, total)
    remote(stz_send, stz_r, STATZ, to_half).start()
    mixz_send[...] = jnp.concatenate(acc, axis=0).astype(BF16)
    remote(mixz_send, mixz_r, MIXZ, to_half).start()
    top, total, acc = combine_y(z_hi)
    own_st = packed(top, total)
    own_mix = jnp.concatenate(acc, axis=0)

    landed(ag2_c, DOWNC)
    od[1 - core] = down[1 - core] + step_size * (adapter_scale * tiles_of(ag2_c))
    store_down = pltpu.make_async_copy(od, od_h, out_sem.at[0])
    store_down.start()
    landed(agu_c, UPC)
    new_up_c = up_updated(1 - core, agu_c[...])
    ou[1 - core] = new_up_c
    store_up = pltpu.make_async_copy(ou, ou_h, out_sem.at[1])
    store_up.start()

    landed(upx_r, UPX)
    even = lax.rem(tp, 2) == 0

    def both(mine, theirs):
        left = jnp.where(even, mine, theirs)
        right = jnp.where(even, theirs, mine)
        return jnp.concatenate([left, right], axis=1)

    def columns(mine, theirs):
        return both(mine, unfold(theirs.reshape(32, 128)).astype(F32)).astype(BF16)

    up_own = columns(new_up, upx_r[0])
    up_oth = columns(new_up_c, upx_r[1])
    landed(basep_r, BASEP)
    base_k = both(base[:, :RANK], basep_r[:, :RANK])
    base_v = both(base[:, RANK:], basep_r[:, RANK:])

    landed(stz_r, STATZ)
    landed(mixz_r, MIXZ)
    top, total, acc = combine(
        lambda s: stz_r[...] if s else own_st, lambda s: mixz_r[...] if s else own_mix, 2
    )
    old_high = jnp.concatenate([top[:, i : i + 1] for i in range(ROWS)], axis=0)
    old_total = jnp.concatenate([total[:, i : i + 1] for i in range(ROWS)], axis=0)
    old_mix = jnp.concatenate(acc, axis=0)
    own_q = qp[:, pl.ds(pl.multiple_of(8 * tp, 8), 8), :].reshape(64, HD).astype(BF16)

    landed(low_r.at[pl.ds(1, 2 * N_TP - 1)], LOW)

    low_own = unfold(summed(low_send[0].astype(F32), low_r, 1, N_TP)).astype(BF16)
    low_oth = unfold(summed(jnp.zeros((16, 128), F32), low_r, N_TP, 2 * N_TP)).astype(BF16)
    from_own = adapter_scale * dot(low_own, up_own)
    from_oth = adapter_scale * dot(low_oth, up_oth)
    first = core == 0
    new_k = (base_k + jnp.where(first, from_own, from_oth)).astype(BF16)
    new_v = (base_v + jnp.where(first, from_oth, from_own)).astype(BF16)
    row = iota((64, 32), 0)
    col = iota((64, 32), 1)
    causal = jnp.logical_and(
        lax.div(row, 8) == lax.div(col, STEPS), lax.rem(col, STEPS) <= lax.rem(row, STEPS)
    )
    score = jnp.where(causal, dot_nt(own_q, new_k) * score_scale, masked_score)
    new_high = jnp.max(score, axis=1, keepdims=True)
    weight = jnp.where(causal, jnp.exp(score - new_high), 0.0)
    new_total = jnp.sum(weight, axis=1, keepdims=True)
    new_mix = dot(weight.astype(BF16), new_v)
    highest = jnp.maximum(old_high, new_high)
    f_old = jnp.exp(old_high - highest)
    f_new = jnp.exp(new_high - highest)
    out = (f_old * old_mix + f_new * new_mix) / (f_old * old_total + f_new * new_total)
    out = out.reshape(ROWS, 8, HD)
    oa[:, :, 0:HD] = out[:, 0:STEPS].astype(BF16)
    oa[:, :, HD:] = out[:, STEPS:].astype(BF16)
    store_att = pltpu.make_async_copy(oa, oa_h, out_sem.at[2])
    store_att.start()

    for ref, chan in (
        (rs1.at[0], RS1B),
        (rs1.at[1], RS1P),
        (ag1.at[0], AG1B),
        (ag1.at[1], AG1P),
        (x_c, XC),
        (wt_c, WC),
        (hid_c, HC),
        (rs2, RS2),
        (rs2, AG2),
        (base_r, BASEY),
        (basez_r, BASEZ),
        (basep_r, BASEP),
        (mix_r, MIXY),
        (st_r, STATY),
        (mixz_r, MIXZ),
        (stz_r, STATZ),
        (low_r.at[pl.ds(1, 2 * N_TP - 1)], LOW),
        (ag2_c, DOWNC),
        (agu_c, UPC),
        (upx_r, UPX),
    ):
        sent(ref, chan)

    @pl.when(is_owner)
    def _():
        sent(agu.at[0], RS2U)
        sent(rs2u, AG2U)

    @pl.when(jnp.logical_not(is_owner))
    def _():
        sent(agu, RS2U)

    store_down.wait()
    store_up.wait()
    store_att.wait()


def shards(
    learn_input,
    cotangent,
    rewards,
    group_ids,
    adapter_down,
    adapter_up,
    frozen_weight,
    hidden,
    queries,
    key_cache,
    value_cache,
    cache_lengths,
):
    hbm = pl.BlockSpec(memory_space=pltpu.HBM)
    operands = (
        learn_input,
        jnp.transpose(cotangent, (1, 2, 0)).reshape(128, TOK),
        adapter_down,
        adapter_up,
        hidden,
        frozen_weight,
        queries.reshape(ROWS, 128, HD),
        key_cache.reshape(ROWS, CACHE_DEV * KVH, HD),
        value_cache.reshape(ROWS, CACHE_DEV * KVH, HD),
    )
    out_shape = (
        jax.ShapeDtypeStruct((2, RANK, FEAT), F32),
        jax.ShapeDtypeStruct((2, RANK, RANK), F32),
        jax.ShapeDtypeStruct((ROWS, STEPS, 2 * HD), BF16),
    )
    return pl.pallas_call(
        kernel,
        out_shape=out_shape,
        in_specs=[hbm] * 12,
        out_specs=(hbm,) * 3,
        scratch_shapes=[
            pltpu.SMEM((SEQ_DEV,), F32),
            pltpu.SMEM((SEQ_DEV,), jnp.int32),
            pltpu.SMEM((ROWS,), jnp.int32),
        ]
        + [pltpu.VMEM(o.shape, o.dtype) for o in operands + out_shape]
        + [
            pltpu.VMEM((TOK, FEAT), BF16),
            pltpu.VMEM((2, RANK, TOK), BF16),
            pltpu.VMEM((RANK, TOK), BF16),
            pltpu.VMEM((ROWS, STEPS, FEAT), BF16),
            pltpu.VMEM((ROWS * STEPS, FEAT), F32),
            pltpu.VMEM((2, 16, 16, 128), BF16),
            pltpu.VMEM((2, 16, 16, 128), BF16),
            pltpu.VMEM((2, 16, 128), BF16),
            pltpu.VMEM((2, 2, 4, 2, 16, 128), BF16),
            pltpu.VMEM((16, 16, 128), BF16),
            pltpu.VMEM((15, 16, 128), BF16),
            pltpu.VMEM((16, 16, 128), BF16),
            pltpu.VMEM((16, 16, 128), BF16),
            pltpu.VMEM((2, 16, 128), BF16),
            pltpu.VMEM((15, 16, 128), BF16),
            pltpu.VMEM((2, 16, 128), BF16),
            pltpu.VMEM((2, 16, 128), BF16),
            pltpu.VMEM((16, 32, 128), BF16),
            pltpu.VMEM((7, 2, 32, 128), BF16),
            pltpu.VMEM((32, 128), F32),
            pltpu.VMEM((32, 128), F32),
            pltpu.VMEM((32, 128), F32),
            pltpu.VMEM((32, 128), F32),
            pltpu.VMEM((16, 64, HD), BF16),
            pltpu.VMEM((7, 2, 64, HD), BF16),
            pltpu.VMEM((64, HD), BF16),
            pltpu.VMEM((64, HD), BF16),
            pltpu.VMEM((16, 8, 128), F32),
            pltpu.VMEM((7, 2, 8, 128), F32),
            pltpu.VMEM((8, 128), F32),
            pltpu.VMEM((8, 128), F32),
            pltpu.VMEM((2, 16, 128), BF16),
            pltpu.VMEM((32, 16, 128), BF16),
            pltpu.VMEM((2, 16, 128), BF16),
            pltpu.VMEM((2, 2, 16, 128), BF16),
            pltpu.VMEM((ROWS, 128, HD), F32),
            pltpu.SemaphoreType.DMA((12,)),
            pltpu.SemaphoreType.DMA((3,)),
            pltpu.SemaphoreType.DMA((N_CHAN,)),
            pltpu.SemaphoreType.DMA((N_CHAN,)),
        ],
        compiler_params=pltpu.CompilerParams(
            collective_id=0, has_side_effects=True, vmem_limit_bytes=VMEM_LIMIT
        ),
    )(rewards, group_ids, cache_lengths, *operands)


def solution(mesh):
    return jax.shard_map(
        shards,
        mesh=mesh,
        in_specs=(
            P("dp", "tensor"),
            P("dp", None, "tensor"),
            P("dp"),
            P("dp"),
            P(None, None, "tensor"),
            P(None, None, "tensor"),
            P(None, "tensor", None),
            P("dp", None, "tensor"),
            P("dp", None, None, None),
            P("dp", "tensor", None, None),
            P("dp", "tensor", None, None),
            P("dp"),
        ),
        out_specs=(P(None, None, "tensor"), P(None, None, "tensor"), P("dp", None, "tensor")),
        check_vma=False,
    )
```

time: 75.8 us -> 55.2 us (0.73)
  Pallas kernels: 61.6 us -> 49.9 us
  local copies, waits for them, and re-layouts: 13 us -> 4.47 us
    pallas_call x1, Pallas kernels: 61.6 us -> 49.9 us  [shards(): pl.pallas_call(kernel, out_shape=out_shape, in_specs=[hbm] * 12, out_spec...]
    unnamed x27 -> x3, local copies, waits for them, and re-layouts: 13 us -> 4.47 us
where the time goes in v2:
time: 55.2 us; the launch traced here: 55 us
  Pallas kernels  49.9 us (90%)
  local copies, waits for them, and re-layouts  4.47 us (8%)
  between operations  0.64 us (1%)
    pallas_call x1, Pallas kernels, shards(): pl.pallas_call(kernel, out_shape=out_shape, in_specs=[hbm] * 12, out_spec...  49.9 us
    unnamed x3, local copies, waits for them, and re-layouts  4.47 us

profile of v2, /device:TPU:1, one launch (start us, length us, event | category | flops | bytes accessed | tf_op | source)
XLA Modules:
  0.0 55.0 jit_solution(15794742058938367474)
XLA Ops:
  0.6 49.9 %shard_map.139 = (f32[2,64,512]{2,1,0:T(8,128)}, f32[2,64,64]{2,1,0:T(8,128)}, bf16[8,4,256]{2,1,0:T(4,128)(2,1)}) custom-call(f32[8]{0:T(128)} %rew_h.1, s32[8]{0:T(128)} %gid_h.1, s32[8]{0:T(128)} %len_h.1, bf16[256,512]{1,0:T(8,128)(2,1)} %x_h.1, bf16[128,256]{1,0:T(8,128)(2,1)} %bitcast.9, f32[2,64,512]{2,1,0:T(8,128)} %down_h.1, f32[2,64,64]{2,1,0:T(8,128)} %up_h.1, ...), custom_call_target="tpu_custom_call" | custom-call | tf_op jit(solution)/shard_map/pallas_call | solution.py:651
  50.5 1.7 %copy.18 = f32[2,64,512]{2,1,0:T(8,128)} copy(f32[2,64,512]{2,1,0:T(8,128)} %get-tuple-element.6) | data formatting | bytes 524288
  52.2 1.5 %copy.19 = f32[2,64,64]{2,1,0:T(8,128)} copy(f32[2,64,64]{2,1,0:T(8,128)} %get-tuple-element.7) | data formatting | bytes 65536
  53.7 1.3 %copy.20 = bf16[8,4,256]{2,1,0:T(4,128)(2,1)} copy(bf16[8,4,256]{2,1,0:T(4,128)(2,1)} %get-tuple-element.8) | data formatting | bytes 32768

commit v3 on v2

--- a/solution.py
+++ b/solution.py
@@ -25,7 +25,7 @@
 KVH = 8
 HD = 128
 UP_OWNERS = (5, 10)
-VMEM_LIMIT = 60 * 1024 * 1024
+VMEM_LIMIT = 32 * 1024 * 1024
 
 adapter_scale = 2.0
 step_size = 0.004
@@ -100,9 +100,9 @@
     q_h,
     k_h,
     v_h,
-    od_h,
-    ou_h,
-    oa_h,
+    od,
+    ou,
+    oa,
     rew,
     gid,
     lens,
@@ -115,9 +115,6 @@
     qry,
     key,
     val,
-    od,
-    ou,
-    oa,
     x_c,
     wt,
     wt_c,
@@ -155,7 +152,6 @@
     upx_r,
     qp,
     in_sem,
-    out_sem,
     send,
     recv,
 ):
@@ -170,30 +166,26 @@
     pair = tp + 1 - 2 * lax.rem(tp, 2)
     other_half = y + N_Y * (1 - z_hi)
 
-    barrier = pltpu.get_barrier_semaphore()
-
-    def greet(device):
-        pl.semaphore_signal(barrier, inc=1, device_id=device, device_id_type=MESH)
-
-    def greet_middle(s, c):
-        t = lax.rem(tp + s, N_TP)
-        greet({"dp": middle + core, "tensor": t})
-        greet({"dp": middle + 1 - core, "tensor": t})
-        return c
-
-    def greet_chips(s, c):
-        greet({"dp": 2 * lax.rem(chip + s, N_CHIP) + core})
-        return c
-
-    lax.fori_loop(0, N_TP, greet_middle, 0)
-    lax.fori_loop(1, N_CHIP, greet_chips, 0)
-    greet({"dp": other_core})
-
     hbm = (rew_h, gid_h, cot_h, up_h, x_h, down_h, hid_h, fro_h, len_h, q_h, k_h, v_h)
     own = (rew, gid, cot, up, x, down, hid, fro, lens, qry, key, val)
     loads = [pltpu.make_async_copy(h, v, in_sem.at[n]) for n, (h, v) in enumerate(zip(hbm, own))]
     for load in loads:
         load.start()
+
+    ys = [lax.rem(y + o, N_Y) for o in (4, 3, 5, 2, 6, 1, 7, 0)]
+    tps = [N_Y * h + t for t in ys for h in (1 - z_hi, z_hi)]
+    chips = [lax.rem(chip + o, N_CHIP) for o in (8, 7, 9, 6, 10, 5, 11, 4, 12, 3, 13, 2, 14, 1, 15)]
+
+    barrier = pltpu.get_barrier_semaphore()
+
+    def greet(device):
+        pl.semaphore_signal(barrier, inc=1, device_id=device, device_id_type=MESH)
+
+    for t in tps:
+        greet({"dp": middle + core, "tensor": t})
+    for q in chips:
+        greet({"dp": 2 * q + core})
+    greet({"dp": other_core})
 
     def remote(src, dst, chan, device):
         return pltpu.make_async_remote_copy(
@@ -204,13 +196,6 @@
             device_id=device,
             device_id_type=MESH,
         )
-
-    def each(first, last, step):
-        def body(s, c):
-            step(s)
-            return c
-
-        lax.fori_loop(first, last, body, 0)
 
     def landed(ref, chan):
         pltpu.make_async_copy(ref, ref, recv.at[chan]).wait()
@@ -256,22 +241,21 @@
     for k in range(2):
         wt[k] = (cot[RANK * k : RANK * (k + 1)].astype(F32) * token_weight).astype(BF16)
         put_pieces(0, k, dot(up[k].astype(BF16), wt[k]))
+
+    pl.semaphore_wait(barrier, N_TP + N_CHIP)
+
+    def send_pieces(part, chan):
+        for s, t in enumerate(tps):
+            device = {"dp": middle + core, "tensor": t}
+            remote(pb_send.at[part, t], rs1.at[part, s], chan, device).start()
+
+    send_pieces(0, RS1B)
     loads[X].wait()
     loads[DOWN].wait()
     for k in range(2):
         put_pieces(1, k, dot_nt(down[k].astype(BF16), x[...]))
+    send_pieces(1, RS1P)
     loads[HID].wait()
-
-    pl.semaphore_wait(barrier, 2 * N_TP + N_CHIP)
-
-    for part, chan in ((0, RS1B), (1, RS1P)):
-
-        def send_piece(s, part=part, chan=chan):
-            t = lax.rem(tp + s, N_TP)
-            device = {"dp": middle + core, "tensor": t}
-            remote(pb_send.at[part, t], rs1.at[part, s], chan, device).start()
-
-        each(0, N_TP, send_piece)
     to_core = {"dp": other_core}
     remote(wt.at[1 - core], wt_c, WC, to_core).start()
     remote(x, x_c, XC, to_core).start()
@@ -333,14 +317,16 @@
     for part, chan_in, chan_out in ((0, RS1B, AG1B), (1, RS1P, AG1P)):
         landed(rs1.at[part], chan_in)
         ag1_send[part] = summed(jnp.zeros((16, 128), F32), rs1.at[part], 0, N_TP).astype(BF16)
-
-        def send_sum(s, part=part, chan=chan_out):
-            device = {"dp": middle + owned_k, "tensor": lax.rem(tp + s, N_TP)}
-            remote(
-                ag1_send.at[part], ag1.at[part, core, owned_r, owned_half], chan, device
-            ).start()
-
-        each(0, N_TP, send_sum)
+        for t in tps:
+            device = {"dp": middle + owned_k, "tensor": t}
+            place = ag1.at[part, core, owned_r, owned_half]
+            remote(ag1_send.at[part], place, chan_out, device).start()
+
+    for s, to in enumerate(ys[:-1]):
+        for z in range(2):
+            t = N_Y * z + to
+            device = {"tensor": N_Y * z_hi + to}
+            remote(base_send.at[t], base_r.at[s, z], BASEY, device).start()
 
     landed(x_c, XC)
     landed(wt_c, WC)
@@ -354,11 +340,15 @@
         r, c = n // 4, n % 4
         g_send[n] = g_down[16 * r : 16 * (r + 1), 128 * c : 128 * (c + 1)]
 
-    def send_tile(s):
-        q = lax.rem(chip + s, N_CHIP)
-        remote(g_send.at[q], rs2.at[s - 1], RS2, {"dp": 2 * q + core}).start()
-
-    each(1, N_CHIP, send_tile)
+    for s, q in enumerate(chips):
+        remote(g_send.at[q], rs2.at[s], RS2, {"dp": 2 * q + core}).start()
+
+    for s, to in enumerate(ys[:-1]):
+        for z in range(2):
+            t = N_Y * z + to
+            device = {"tensor": N_Y * z_hi + to}
+            remote(st_send.at[t], st_r.at[s, z], STATY, device).start()
+            remote(mix_send.at[t], mix_r.at[s, z], MIXY, device).start()
 
     landed(ag1.at[1], AG1P)
 
@@ -371,23 +361,6 @@
             slot = lax.rem(q - chip + N_CHIP, N_CHIP) - 1
             remote(gu_send.at[u], rs2u.at[slot], RS2U, {"dp": 2 * q + core}).start()
 
-    def send_along_y(s):
-        to = lax.rem(y + s, N_Y)
-        device = {"tensor": N_Y * z_hi + to}
-        for z in range(2):
-            t = N_Y * z + to
-            remote(base_send.at[t], base_r.at[s - 1, z], BASEY, device).start()
-
-    def send_mix_along_y(s):
-        to = lax.rem(y + s, N_Y)
-        device = {"tensor": N_Y * z_hi + to}
-        for z in range(2):
-            t = N_Y * z + to
-            remote(st_send.at[t], st_r.at[s - 1, z], STATY, device).start()
-            remote(mix_send.at[t], mix_r.at[s - 1, z], MIXY, device).start()
-
-    each(1, N_Y, send_along_y)
-    each(1, N_Y, send_mix_along_y)
     for i in range(ROWS):
         hid_f[STEPS * i : STEPS * (i + 1), :] = hid_c[i].astype(F32)
     hid_cb = hid_f[...].astype(BF16)
@@ -396,11 +369,8 @@
 
     ag2[chip] = summed(g_send[chip].astype(F32), rs2, 0, N_CHIP - 1).astype(BF16)
 
-    def send_total(s):
-        q = lax.rem(chip + s, N_CHIP)
+    for q in chips:
         remote(ag2.at[chip], ag2.at[chip], AG2, {"dp": 2 * q + core}).start()
-
-    each(1, N_CHIP, send_total)
 
     is_owner = jnp.logical_or(chip == UP_OWNERS[0], chip == UP_OWNERS[1])
     up_tile = jnp.where(chip == UP_OWNERS[0], 0, 1)
@@ -409,12 +379,8 @@
     def _():
         landed(rs2u, RS2U)
         agu[up_tile] = summed(gu_send[up_tile].astype(F32), rs2u, 0, N_CHIP - 1).astype(BF16)
-
-        def send_up(s):
-            q = lax.rem(chip + s, N_CHIP)
+        for q in chips:
             remote(agu.at[up_tile], agu.at[up_tile], AG2U, {"dp": 2 * q + core}).start()
-
-        each(1, N_CHIP, send_up)
 
     landed(base_r, BASEY)
 
@@ -441,15 +407,11 @@
     low_send[0] = fold(dot_nt(hid_b, roll_down)).astype(BF16)
     low_send[1] = fold(dot_nt(hid_cb, roll_down)).astype(BF16)
 
-    def send_low(s):
-        t = lax.rem(tp + s, N_TP)
-        remote(low_send.at[0], low_r.at[s], LOW, {"tensor": t}).start()
-        remote(
-            low_send.at[1], low_r.at[N_TP + s], LOW, {"dp": other_core, "tensor": t}
-        ).start()
-
-    each(1, N_TP, send_low)
-    remote(low_send.at[1], low_r.at[N_TP], LOW, to_core).start()
+    for s, t in enumerate(tps):
+        if s < N_TP - 1:
+            remote(low_send.at[0], low_r.at[s], LOW, {"tensor": t}).start()
+        device = {"dp": other_core, "tensor": t}
+        remote(low_send.at[1], low_r.at[N_TP - 1 + s], LOW, device).start()
     remote(ag2, ag2_c, DOWNC, to_core).start()
     od[core] = new_down
 
@@ -515,13 +477,9 @@
 
     landed(ag2_c, DOWNC)
     od[1 - core] = down[1 - core] + step_size * (adapter_scale * tiles_of(ag2_c))
-    store_down = pltpu.make_async_copy(od, od_h, out_sem.at[0])
-    store_down.start()
     landed(agu_c, UPC)
     new_up_c = up_updated(1 - core, agu_c[...])
     ou[1 - core] = new_up_c
-    store_up = pltpu.make_async_copy(ou, ou_h, out_sem.at[1])
-    store_up.start()
 
     landed(upx_r, UPX)
     even = lax.rem(tp, 2) == 0
@@ -550,10 +508,10 @@
     old_mix = jnp.concatenate(acc, axis=0)
     own_q = qp[:, pl.ds(pl.multiple_of(8 * tp, 8), 8), :].reshape(64, HD).astype(BF16)
 
-    landed(low_r.at[pl.ds(1, 2 * N_TP - 1)], LOW)
-
-    low_own = unfold(summed(low_send[0].astype(F32), low_r, 1, N_TP)).astype(BF16)
-    low_oth = unfold(summed(jnp.zeros((16, 128), F32), low_r, N_TP, 2 * N_TP)).astype(BF16)
+    landed(low_r, LOW)
+
+    low_own = unfold(summed(low_send[0].astype(F32), low_r, 0, N_TP - 1)).astype(BF16)
+    low_oth = unfold(summed(jnp.zeros((16, 128), F32), low_r, N_TP - 1, 2 * N_TP - 1)).astype(BF16)
     from_own = adapter_scale * dot(low_own, up_own)
     from_oth = adapter_scale * dot(low_oth, up_oth)
     first = core == 0
@@ -576,8 +534,6 @@
     out = out.reshape(ROWS, 8, HD)
     oa[:, :, 0:HD] = out[:, 0:STEPS].astype(BF16)
     oa[:, :, HD:] = out[:, STEPS:].astype(BF16)
-    store_att = pltpu.make_async_copy(oa, oa_h, out_sem.at[2])
-    store_att.start()
 
     for ref, chan in (
         (rs1.at[0], RS1B),
@@ -596,7 +552,7 @@
         (st_r, STATY),
         (mixz_r, MIXZ),
         (stz_r, STATZ),
-        (low_r.at[pl.ds(1, 2 * N_TP - 1)], LOW),
+        (low_r, LOW),
         (ag2_c, DOWNC),
         (agu_c, UPC),
         (upx_r, UPX),
@@ -611,10 +567,6 @@
     @pl.when(jnp.logical_not(is_owner))
     def _():
         sent(agu, RS2U)
-
-    store_down.wait()
-    store_up.wait()
-    store_att.wait()
 
 
 def shards(
@@ -648,17 +600,18 @@
         jax.ShapeDtypeStruct((2, RANK, RANK), F32),
         jax.ShapeDtypeStruct((ROWS, STEPS, 2 * HD), BF16),
     )
+    vmem = pl.BlockSpec(memory_space=pltpu.VMEM)
     return pl.pallas_call(
         kernel,
         out_shape=out_shape,
         in_specs=[hbm] * 12,
-        out_specs=(hbm,) * 3,
+        out_specs=(vmem,) * 3,
         scratch_shapes=[
             pltpu.SMEM((SEQ_DEV,), F32),
             pltpu.SMEM((SEQ_DEV,), jnp.int32),
             pltpu.SMEM((ROWS,), jnp.int32),
         ]
-        + [pltpu.VMEM(o.shape, o.dtype) for o in operands + out_shape]
+        + [pltpu.VMEM(o.shape, o.dtype) for o in operands]
         + [
             pltpu.VMEM((TOK, FEAT), BF16),
             pltpu.VMEM((2, RANK, TOK), BF16),
@@ -692,19 +645,23 @@
             pltpu.VMEM((8, 128), F32),
             pltpu.VMEM((8, 128), F32),
             pltpu.VMEM((2, 16, 128), BF16),
-            pltpu.VMEM((32, 16, 128), BF16),
+            pltpu.VMEM((31, 16, 128), BF16),
             pltpu.VMEM((2, 16, 128), BF16),
             pltpu.VMEM((2, 2, 16, 128), BF16),
             pltpu.VMEM((ROWS, 128, HD), F32),
             pltpu.SemaphoreType.DMA((12,)),
-            pltpu.SemaphoreType.DMA((3,)),
             pltpu.SemaphoreType.DMA((N_CHAN,)),
             pltpu.SemaphoreType.DMA((N_CHAN,)),
         ],
         compiler_params=pltpu.CompilerParams(
             collective_id=0, has_side_effects=True, vmem_limit_bytes=VMEM_LIMIT
         ),
-    )(rewards, group_ids, cache_lengths, *operands)
+    )(
+        *(
+            pltpu.with_memory_space_constraint(o, pltpu.HBM)
+            for o in (rewards, group_ids, cache_lengths, *operands)
+        )
+    )
 
 
 def solution(mesh):

time: 55.2 us -> 51.2 us (0.928)
  local copies, waits for them, and re-layouts: 4.47 us -> 1.94 us
  Pallas kernels: 49.9 us -> 48.5 us
    unnamed x3, local copies, waits for them, and re-layouts: 4.47 us -> 1.94 us
    pallas_call x1, Pallas kernels: 49.9 us -> 48.5 us  [shards(): pl.pallas_call(kernel, out_shape=out_shape, in_specs=[hbm] * 12, out_spec...]
where the time goes in v3:
time: 51.2 us; the launch traced here: 51.1 us
  Pallas kernels  48.5 us (95%)
  local copies, waits for them, and re-layouts  1.94 us (4%)
  between operations  0.64 us (1%)
    pallas_call x1, Pallas kernels, shards(): pl.pallas_call(kernel, out_shape=out_shape, in_specs=[hbm] * 12, out_spec...  48.5 us
    unnamed x3, local copies, waits for them, and re-layouts  1.94 us

profile of v3, /device:TPU:1, one launch (start us, length us, event | category | flops | bytes accessed | tf_op | source)
XLA Modules:
  0.0 51.1 jit_solution(6658589630327373123)
XLA Ops:
  0.6 48.5 %shard_map.139 = (f32[2,64,512]{2,1,0:T(8,128)S(1)}, f32[2,64,64]{2,1,0:T(8,128)S(1)}, bf16[8,4,256]{2,1,0:T(4,128)(2,1)S(1)}) custom-call(f32[8]{0:T(128)} %rew_h.1, s32[8]{0:T(128)} %gid_h.1, s32[8]{0:T(128)} %len_h.1, bf16[256,512]{1,0:T(8,128)(2,1)} %x_h.1, bf16[128,256]{1,0:T(8,128)(2,1)} %bitcast.9, f32[2,64,512]{2,1,0:T(8,128)} %down_h.1, ...), custom_call_target="tpu_custom_call" | custom-call | tf_op jit(solution)/shard_map/pallas_call | solution.py:604
  49.1 0.7 %copy.18 = f32[2,64,512]{2,1,0:T(8,128)} copy(f32[2,64,512]{2,1,0:T(8,128)S(1)} %get-tuple-element.6) | data formatting | bytes 524288
  49.8 0.6 %copy.19 = f32[2,64,64]{2,1,0:T(8,128)} copy(f32[2,64,64]{2,1,0:T(8,128)S(1)} %get-tuple-element.7) | data formatting | bytes 65536
  50.5 0.6 %copy.20 = bf16[8,4,256]{2,1,0:T(4,128)(2,1)} copy(bf16[8,4,256]{2,1,0:T(4,128)(2,1)S(1)} %get-tuple-element.8) | data formatting | bytes 32768

commit v4 on v3

--- a/solution.py
+++ b/solution.py
@@ -24,7 +24,6 @@
 CACHE_DEV = 48
 KVH = 8
 HD = 128
-UP_OWNERS = (5, 10)
 VMEM_LIMIT = 32 * 1024 * 1024
 
 adapter_scale = 2.0
@@ -40,7 +39,11 @@
     AG1P,
     XC,
     WC,
-    HC,
+    HZ,
+    HX,
+    HC1,
+    HC2,
+    LRS,
     RS2,
     RS2U,
     AG2,
@@ -57,7 +60,7 @@
     UPC,
     UPX,
     N_CHAN,
-) = range(23)
+) = range(27)
 
 
 def dot(a, b):
@@ -118,8 +121,11 @@
     x_c,
     wt,
     wt_c,
-    hid_c,
     hid_f,
+    h_all,
+    h_down,
+    l_send,
+    l_r,
     pb_send,
     rs1,
     ag1_send,
@@ -161,7 +167,12 @@
     core = lax.rem(dp, 2)
     z_hi = lax.div(tp, N_Y)
     y = lax.rem(tp, N_Y)
-    middle = 2 * (chip + 2 - 4 * lax.rem(lax.div(chip, 2), 2))
+    def two_along_z(q):
+        return q + 2 - 4 * lax.rem(lax.div(q, 2), 2)
+
+    middle = 2 * two_along_z(chip)
+    column = 4 * lax.div(chip, 4)
+    z_lo = lax.rem(chip, 4)
     other_core = 2 * chip + 1 - core
     pair = tp + 1 - 2 * lax.rem(tp, 2)
     other_half = y + N_Y * (1 - z_hi)
@@ -176,6 +187,10 @@
     tps = [N_Y * h + t for t in ys for h in (1 - z_hi, z_hi)]
     chips = [lax.rem(chip + o, N_CHIP) for o in (8, 7, 9, 6, 10, 5, 11, 4, 12, 3, 13, 2, 14, 1, 15)]
 
+    sheet = [(q, h) for q in chips + [chip] for h in (1 - z_hi, z_hi)][:-1]
+    z_near = [column + lax.rem(z_lo + o, 4) for o in (2, 1, 3)]
+    x_near = [lax.rem(chip + 4 * o, N_CHIP) for o in (2, 1, 3)]
+
     barrier = pltpu.get_barrier_semaphore()
 
     def greet(device):
@@ -183,8 +198,8 @@
 
     for t in tps:
         greet({"dp": middle + core, "tensor": t})
-    for q in chips:
-        greet({"dp": 2 * q + core})
+    for q, h in sheet:
+        greet({"dp": 2 * q + core, "tensor": N_Y * h + y})
     greet({"dp": other_core})
 
     def remote(src, dst, chan, device):
@@ -242,7 +257,7 @@
         wt[k] = (cot[RANK * k : RANK * (k + 1)].astype(F32) * token_weight).astype(BF16)
         put_pieces(0, k, dot(up[k].astype(BF16), wt[k]))
 
-    pl.semaphore_wait(barrier, N_TP + N_CHIP)
+    pl.semaphore_wait(barrier, N_TP + 2 * N_CHIP)
 
     def send_pieces(part, chan):
         for s, t in enumerate(tps):
@@ -255,15 +270,21 @@
     for k in range(2):
         put_pieces(1, k, dot_nt(down[k].astype(BF16), x[...]))
     send_pieces(1, RS1P)
-    loads[HID].wait()
     to_core = {"dp": other_core}
     remote(wt.at[1 - core], wt_c, WC, to_core).start()
     remote(x, x_c, XC, to_core).start()
-    remote(hid, hid_c, HC, to_core).start()
-
+
+    loads[HID].wait()
     for i in range(ROWS):
         hid_f[STEPS * i : STEPS * (i + 1), :] = hid[i].astype(F32)
     hid_b = hid_f[...].astype(BF16)
+    h_all[core, chip] = hid_b
+    rows = h_all.at[core, chip]
+    for q in z_near:
+        remote(rows, rows, HZ, {"dp": 2 * q + core}).start()
+    for q in x_near:
+        remote(rows, rows, HX, {"dp": 2 * q + core}).start()
+
     loads[FRO].wait()
     for part in range(4):
         cols = slice(part * 256, (part + 1) * 256)
@@ -321,6 +342,14 @@
             device = {"dp": middle + owned_k, "tensor": t}
             place = ag1.at[part, core, owned_r, owned_half]
             remote(ag1_send.at[part], place, chan_out, device).start()
+        if part == 0:
+            landed(h_all.at[0, pl.ds(0, 3)], HZ)
+            for q in x_near:
+                for n in z_near:
+                    rows = h_all.at[core, n]
+                    remote(rows, rows, HX, {"dp": 2 * q + core}).start()
+            rows = h_all.at[core, pl.ds(column, 4)]
+            remote(rows, rows, HC1, to_core).start()
 
     for s, to in enumerate(ys[:-1]):
         for z in range(2):
@@ -330,18 +359,10 @@
 
     landed(x_c, XC)
     landed(wt_c, WC)
-    landed(hid_c, HC)
-
-    landed(ag1.at[0], AG1B)
-
-    g_down = dot(by_tiles(ag1[0, core]), x[...]) + dot(by_tiles(ag1[0, 1 - core]), x_c[...])
-    g_down = g_down.astype(BF16)
-    for n in range(N_CHIP):
-        r, c = n // 4, n % 4
-        g_send[n] = g_down[16 * r : 16 * (r + 1), 128 * c : 128 * (c + 1)]
-
-    for s, q in enumerate(chips):
-        remote(g_send.at[q], rs2.at[s], RS2, {"dp": 2 * q + core}).start()
+    landed(h_all.at[0, pl.ds(0, 4)], HC1)
+    down_b = down[core].astype(BF16)
+    for c in range(2):
+        h_down[c] = fold(dot_nt(h_all[c, chip], down_b))
 
     for s, to in enumerate(ys[:-1]):
         for z in range(2):
@@ -350,37 +371,45 @@
             remote(st_send.at[t], st_r.at[s, z], STATY, device).start()
             remote(mix_send.at[t], mix_r.at[s, z], MIXY, device).start()
 
+    landed(ag1.at[0], AG1B)
+
+    landed(h_all.at[0, pl.ds(0, 12)], HX)
+    for q in x_near:
+        rows = h_all.at[core, pl.ds(4 * lax.div(q, 4), 4)]
+        remote(rows, rows, HC2, to_core).start()
+
+    g_down = dot(by_tiles(ag1[0, core]), x[...]) + dot(by_tiles(ag1[0, 1 - core]), x_c[...])
+    g_down = g_down.astype(BF16)
+    for n in range(N_CHIP):
+        r, c = n // 4, n % 4
+        g_send[n] = g_down[16 * r : 16 * (r + 1), 128 * c : 128 * (c + 1)]
+    for s, q in enumerate(chips):
+        remote(g_send.at[q], rs2.at[s], RS2, {"dp": 2 * q + core}).start()
+
+    def rows_product(c):
+        part = step_size * adapter_scale * dot_nt(h_all[c].reshape(512, FEAT), g_down)
+        part = part.reshape(N_CHIP, 2, 16, RANK)
+        l_send[c] = jnp.concatenate([part[:, 0], part[:, 1]], axis=2).astype(BF16)
+        own = step_size * adapter_scale * fold(dot_nt(h_all[c, chip], g_down))
+        l_send[c, chip] = (own + h_down[c]).astype(BF16)
+
+    rows_product(core)
+
     landed(ag1.at[1], AG1P)
 
     g_up = dot_nt(by_tiles(ag1[1, core]), wt[core]) + dot_nt(by_tiles(ag1[1, 1 - core]), wt_c[...])
-    gu_send[...] = fold(g_up).astype(BF16).reshape(2, 16, 128)
-    for u, q in enumerate(UP_OWNERS):
-
-        @pl.when(chip != q)
-        def _(u=u, q=q):
-            slot = lax.rem(q - chip + N_CHIP, N_CHIP) - 1
-            remote(gu_send.at[u], rs2u.at[slot], RS2U, {"dp": 2 * q + core}).start()
-
-    for i in range(ROWS):
-        hid_f[STEPS * i : STEPS * (i + 1), :] = hid_c[i].astype(F32)
-    hid_cb = hid_f[...].astype(BF16)
-
-    landed(rs2, RS2)
-
-    ag2[chip] = summed(g_send[chip].astype(F32), rs2, 0, N_CHIP - 1).astype(BF16)
-
-    for q in chips:
-        remote(ag2.at[chip], ag2.at[chip], AG2, {"dp": 2 * q + core}).start()
-
-    is_owner = jnp.logical_or(chip == UP_OWNERS[0], chip == UP_OWNERS[1])
-    up_tile = jnp.where(chip == UP_OWNERS[0], 0, 1)
-
-    @pl.when(is_owner)
-    def _():
-        landed(rs2u, RS2U)
-        agu[up_tile] = summed(gu_send[up_tile].astype(F32), rs2u, 0, N_CHIP - 1).astype(BF16)
-        for q in chips:
-            remote(agu.at[up_tile], agu.at[up_tile], AG2U, {"dp": 2 * q + core}).start()
+    g_up = fold(g_up)
+    for n in range(N_CHIP):
+        gu_send[n] = g_up[2 * n : 2 * (n + 1)]
+    for s, q in enumerate(chips):
+        remote(gu_send.at[q], rs2u.at[s], RS2U, {"dp": 2 * q + core}).start()
+
+    landed(h_all.at[0, pl.ds(0, 12)], HC2)
+    rows_product(1 - core)
+
+    for s, (q, h) in enumerate(sheet):
+        device = {"dp": 2 * q + core, "tensor": N_Y * h + y}
+        remote(l_send.at[h, two_along_z(q)], l_r.at[s], LRS, device).start()
 
     landed(base_r, BASEY)
 
@@ -395,48 +424,17 @@
     remote(basez_send, basez_r, BASEZ, to_half).start()
     base = base_sum(z_hi)
 
-    landed(ag2.at[pl.ds(0, N_CHIP - 1)], AG2)
-
-    def tiles_of(ref):
-        return jnp.concatenate(
-            [jnp.concatenate([ref[4 * r + c] for c in range(4)], axis=1) for r in range(4)], axis=0
-        ).astype(F32)
-
-    new_down = down[core] + step_size * (adapter_scale * tiles_of(ag2))
-    roll_down = new_down.astype(BF16)
-    low_send[0] = fold(dot_nt(hid_b, roll_down)).astype(BF16)
-    low_send[1] = fold(dot_nt(hid_cb, roll_down)).astype(BF16)
-
-    for s, t in enumerate(tps):
-        if s < N_TP - 1:
-            remote(low_send.at[0], low_r.at[s], LOW, {"tensor": t}).start()
-        device = {"dp": other_core, "tensor": t}
-        remote(low_send.at[1], low_r.at[N_TP - 1 + s], LOW, device).start()
-    remote(ag2, ag2_c, DOWNC, to_core).start()
-    od[core] = new_down
-
-    @pl.when(is_owner)
-    def _():
-        landed(agu.at[0], AG2U)
-
-    @pl.when(jnp.logical_not(is_owner))
-    def _():
-        landed(agu, AG2U)
-
-    def up_updated(k, grad):
-        return up[k] + step_size * (adapter_scale * unfold(grad.reshape(32, 128)).astype(F32))
-
-    new_up = up_updated(core, agu[...])
-    upx_send[...] = fold(new_up).astype(BF16).reshape(2, 16, 128)
-    remote(agu, agu_c, UPC, to_core).start()
-    remote(upx_send, upx_r.at[0], UPX, {"tensor": pair}).start()
-    remote(upx_send, upx_r.at[1], UPX, {"dp": other_core, "tensor": pair}).start()
-    ou[core] = new_up
-
-    landed(basez_r, BASEZ)
-    base = base + basez_r[...]
-    basep_send[...] = base
-    remote(basep_send, basep_r, BASEP, {"tensor": pair}).start()
+    landed(rs2, RS2)
+
+    ag2[chip] = summed(g_send[chip].astype(F32), rs2, 0, N_CHIP - 1).astype(BF16)
+
+    for q in chips:
+        remote(ag2.at[chip], ag2.at[chip], AG2, {"dp": 2 * q + core}).start()
+
+    landed(rs2u, RS2U)
+    agu[chip] = summed(gu_send[chip], rs2u, 0, N_CHIP - 1)
+    for q in chips:
+        remote(agu.at[chip], agu.at[chip], AG2U, {"dp": 2 * q + core}).start()
 
     landed(st_r, STATY)
     landed(mix_r, MIXY)
@@ -475,6 +473,42 @@
     own_st = packed(top, total)
     own_mix = jnp.concatenate(acc, axis=0)
 
+    landed(l_r, LRS)
+
+    low_send[...] = summed(
+        l_send[z_hi, two_along_z(chip)].astype(F32), l_r, 0, 2 * N_CHIP - 1
+    ).astype(BF16)
+    for t in tps:
+        device = {"dp": middle + z_hi, "tensor": t}
+        remote(low_send, low_r.at[core, y], LOW, device).start()
+
+    landed(basez_r, BASEZ)
+    base = base + basez_r[...]
+    basep_send[...] = base
+    remote(basep_send, basep_r, BASEP, {"tensor": pair}).start()
+
+    landed(ag2.at[pl.ds(0, N_CHIP - 1)], AG2)
+    remote(ag2, ag2_c, DOWNC, to_core).start()
+
+    def tiles_of(ref):
+        return jnp.concatenate(
+            [jnp.concatenate([ref[4 * r + c] for c in range(4)], axis=1) for r in range(4)], axis=0
+        ).astype(F32)
+
+    od[core] = down[core] + step_size * (adapter_scale * tiles_of(ag2))
+
+    landed(agu.at[pl.ds(0, N_CHIP - 1)], AG2U)
+
+    def up_updated(k, grad):
+        return up[k] + step_size * (adapter_scale * unfold(grad.reshape(32, 128)))
+
+    new_up = up_updated(core, agu[...])
+    upx_send[...] = fold(new_up).astype(BF16).reshape(2, 16, 128)
+    remote(agu, agu_c, UPC, to_core).start()
+    remote(upx_send, upx_r.at[0], UPX, {"tensor": pair}).start()
+    remote(upx_send, upx_r.at[1], UPX, {"dp": other_core, "tensor": pair}).start()
+    ou[core] = new_up
+
     landed(ag2_c, DOWNC)
     od[1 - core] = down[1 - core] + step_size * (adapter_scale * tiles_of(ag2_c))
     landed(agu_c, UPC)
@@ -510,8 +544,9 @@
 
     landed(low_r, LOW)
 
-    low_own = unfold(summed(low_send[0].astype(F32), low_r, 0, N_TP - 1)).astype(BF16)
-    low_oth = unfold(summed(jnp.zeros((16, 128), F32), low_r, N_TP - 1, 2 * N_TP - 1)).astype(BF16)
+    none = jnp.zeros((16, 128), F32)
+    low_own = unfold(summed(none, low_r.at[core], 0, N_Y)).astype(BF16)
+    low_oth = unfold(summed(none, low_r.at[1 - core], 0, N_Y)).astype(BF16)
     from_own = adapter_scale * dot(low_own, up_own)
     from_oth = adapter_scale * dot(low_oth, up_oth)
     first = core == 0
@@ -542,7 +577,13 @@
         (ag1.at[1], AG1P),
         (x_c, XC),
         (wt_c, WC),
-        (hid_c, HC),
+        (h_all.at[0, pl.ds(0, 3)], HZ),
+        (h_all.at[0, pl.ds(0, 12)], HX),
+        (h_all.at[0, pl.ds(0, 4)], HC1),
+        (h_all.at[0, pl.ds(0, 12)], HC2),
+        (l_r, LRS),
+        (rs2u, RS2U),
+        (rs2u, AG2U),
         (rs2, RS2),
         (rs2, AG2),
         (base_r, BASEY),
@@ -558,15 +599,6 @@
         (upx_r, UPX),
     ):
         sent(ref, chan)
-
-    @pl.when(is_owner)
-    def _():
-        sent(agu.at[0], RS2U)
-        sent(rs2u, AG2U)
-
-    @pl.when(jnp.logical_not(is_owner))
-    def _():
-        sent(agu, RS2U)
 
 
 def shards(
@@ -616,8 +648,11 @@
             pltpu.VMEM((TOK, FEAT), BF16),
             pltpu.VMEM((2, RANK, TOK), BF16),
             pltpu.VMEM((RANK, TOK), BF16),
-            pltpu.VMEM((ROWS, STEPS, FEAT), BF16),
             pltpu.VMEM((ROWS * STEPS, FEAT), F32),
+            pltpu.VMEM((2, 16, ROWS * STEPS, FEAT), BF16),
+            pltpu.VMEM((2, 16, 128), F32),
+            pltpu.VMEM((2, 16, 16, 128), BF16),
+            pltpu.VMEM((31, 16, 128), BF16),
             pltpu.VMEM((2, 16, 16, 128), BF16),
             pltpu.VMEM((2, 16, 16, 128), BF16),
             pltpu.VMEM((2, 16, 128), BF16),
@@ -626,10 +661,10 @@
             pltpu.VMEM((15, 16, 128), BF16),
             pltpu.VMEM((16, 16, 128), BF16),
             pltpu.VMEM((16, 16, 128), BF16),
-            pltpu.VMEM((2, 16, 128), BF16),
-            pltpu.VMEM((15, 16, 128), BF16),
-            pltpu.VMEM((2, 16, 128), BF16),
-            pltpu.VMEM((2, 16, 128), BF16),
+            pltpu.VMEM((16, 2, 128), F32),
+            pltpu.VMEM((15, 2, 128), F32),
+            pltpu.VMEM((16, 2, 128), F32),
+            pltpu.VMEM((16, 2, 128), F32),
             pltpu.VMEM((16, 32, 128), BF16),
             pltpu.VMEM((7, 2, 32, 128), BF16),
             pltpu.VMEM((32, 128), F32),
@@ -644,8 +679,8 @@
             pltpu.VMEM((7, 2, 8, 128), F32),
             pltpu.VMEM((8, 128), F32),
             pltpu.VMEM((8, 128), F32),
-            pltpu.VMEM((2, 16, 128), BF16),
-            pltpu.VMEM((31, 16, 128), BF16),
+            pltpu.VMEM((16, 128), BF16),
+            pltpu.VMEM((2, 8, 16, 128), BF16),
             pltpu.VMEM((2, 16, 128), BF16),
             pltpu.VMEM((2, 2, 16, 128), BF16),
             pltpu.VMEM((ROWS, 128, HD), F32),

time: 51.2 us -> 49.9 us (0.975)
  Pallas kernels: 48.5 us -> 47.2 us
    pallas_call x1, Pallas kernels: 48.5 us -> 47.2 us  [shards(): pl.pallas_call(kernel, out_shape=out_shape, in_specs=[hbm] * 12, out_spec...]
where the time goes in v4:
time: 49.9 us; the launch traced here: 49.8 us
  Pallas kernels  47.2 us (95%)
  local copies, waits for them, and re-layouts  1.94 us (4%)
  between operations  0.64 us (1%)
    pallas_call x1, Pallas kernels, shards(): pl.pallas_call(kernel, out_shape=out_shape, in_specs=[hbm] * 12, out_spec...  47.2 us
    unnamed x3, local copies, waits for them, and re-layouts  1.94 us

profile of v4, /device:TPU:1, one launch (start us, length us, event | category | flops | bytes accessed | tf_op | source)
XLA Modules:
  0.0 49.8 jit_solution(9209802250106506444)
XLA Ops:
  0.6 47.2 %shard_map.139 = (f32[2,64,512]{2,1,0:T(8,128)S(1)}, f32[2,64,64]{2,1,0:T(8,128)S(1)}, bf16[8,4,256]{2,1,0:T(4,128)(2,1)S(1)}) custom-call(f32[8]{0:T(128)} %rew_h.1, s32[8]{0:T(128)} %gid_h.1, s32[8]{0:T(128)} %len_h.1, bf16[256,512]{1,0:T(8,128)(2,1)} %x_h.1, bf16[128,256]{1,0:T(8,128)(2,1)} %bitcast.9, f32[2,64,512]{2,1,0:T(8,128)} %down_h.1, ...), custom_call_target="tpu_custom_call" | custom-call | tf_op jit(solution)/shard_map/pallas_call | solution.py:636
  47.9 0.7 %copy.18 = f32[2,64,512]{2,1,0:T(8,128)} copy(f32[2,64,512]{2,1,0:T(8,128)S(1)} %get-tuple-element.6) | data formatting | bytes 524288
  48.6 0.6 %copy.19 = f32[2,64,64]{2,1,0:T(8,128)} copy(f32[2,64,64]{2,1,0:T(8,128)S(1)} %get-tuple-element.7) | data formatting | bytes 65536
  49.2 0.6 %copy.20 = bf16[8,4,256]{2,1,0:T(4,128)(2,1)} copy(bf16[8,4,256]{2,1,0:T(4,128)(2,1)S(1)} %get-tuple-element.8) | data formatting | bytes 32768

commit v5 on v4

--- a/solution.py
+++ b/solution.py
@@ -61,6 +61,21 @@
     UPX,
     N_CHAN,
 ) = range(27)
+
+
+TILE = 4
+SENT_BOTH = (
+    2 * 16 * TILE
+    + 32 + 256
+    + (3 + 12 + 4 + 12) * 32
+    + 31 * TILE
+    + 2 * 15 * TILE + 64
+    + 2 * 15 + 16 + 2 * 8
+    + 14 * 8 + 2 * 16
+    + 14 * (16 + TILE) + 16 + TILE
+)
+SENT_0 = SENT_BOTH + TILE
+SENT_1 = SENT_BOTH + 2 * 2 * 16 * TILE + 16 * 2 * TILE
 
 
 def dot(a, b):
@@ -157,6 +172,7 @@
     upx_send,
     upx_r,
     qp,
+    all_sent,
     in_sem,
     send,
     recv,
@@ -187,7 +203,6 @@
     tps = [N_Y * h + t for t in ys for h in (1 - z_hi, z_hi)]
     chips = [lax.rem(chip + o, N_CHIP) for o in (8, 7, 9, 6, 10, 5, 11, 4, 12, 3, 13, 2, 14, 1, 15)]
 
-    sheet = [(q, h) for q in chips + [chip] for h in (1 - z_hi, z_hi)][:-1]
     z_near = [column + lax.rem(z_lo + o, 4) for o in (2, 1, 3)]
     x_near = [lax.rem(chip + 4 * o, N_CHIP) for o in (2, 1, 3)]
 
@@ -196,17 +211,23 @@
     def greet(device):
         pl.semaphore_signal(barrier, inc=1, device_id=device, device_id_type=MESH)
 
-    for t in tps:
-        greet({"dp": middle + core, "tensor": t})
-    for q, h in sheet:
-        greet({"dp": 2 * q + core, "tensor": N_Y * h + y})
+    @pl.when(core == 1)
+    def _():
+        for t in tps:
+            greet({"dp": middle, "tensor": t})
+            greet({"dp": middle + 1, "tensor": t})
+
+    for q in chips:
+        greet({"dp": 2 * q + core})
     greet({"dp": other_core})
+    for t in ys[:-1]:
+        greet({"tensor": N_Y * z_hi + t})
 
     def remote(src, dst, chan, device):
         return pltpu.make_async_remote_copy(
             src_ref=src,
             dst_ref=dst,
-            send_sem=send.at[chan],
+            send_sem=send.at[0],
             recv_sem=recv.at[chan],
             device_id=device,
             device_id_type=MESH,
@@ -215,8 +236,9 @@
     def landed(ref, chan):
         pltpu.make_async_copy(ref, ref, recv.at[chan]).wait()
 
-    def sent(ref, chan):
-        pltpu.make_async_copy(ref, ref, send.at[chan]).wait()
+    def sent(size):
+        ref = all_sent.at[pl.ds(0, size)]
+        pltpu.make_async_copy(ref, ref, send.at[0]).wait()
 
     def summed(first, ref, start, stop):
         return lax.fori_loop(start, stop, lambda s, acc: acc + ref[s].astype(F32), first)
@@ -257,12 +279,12 @@
         wt[k] = (cot[RANK * k : RANK * (k + 1)].astype(F32) * token_weight).astype(BF16)
         put_pieces(0, k, dot(up[k].astype(BF16), wt[k]))
 
-    pl.semaphore_wait(barrier, N_TP + 2 * N_CHIP)
+    pl.semaphore_wait(barrier, N_TP + N_CHIP + N_Y - 1)
 
     def send_pieces(part, chan):
         for s, t in enumerate(tps):
-            device = {"dp": middle + core, "tensor": t}
-            remote(pb_send.at[part, t], rs1.at[part, s], chan, device).start()
+            device = {"dp": middle + 1, "tensor": t}
+            remote(pb_send.at[part, t], rs1.at[part, core, s], chan, device).start()
 
     send_pieces(0, RS1B)
     loads[X].wait()
@@ -335,21 +357,30 @@
     owned_k = lax.div(tp, N_Y)
     owned_r = lax.div(lax.rem(tp, N_Y), 2)
     owned_half = lax.rem(tp, 2)
-    for part, chan_in, chan_out in ((0, RS1B, AG1B), (1, RS1P, AG1P)):
-        landed(rs1.at[part], chan_in)
-        ag1_send[part] = summed(jnp.zeros((16, 128), F32), rs1.at[part], 0, N_TP).astype(BF16)
-        for t in tps:
-            device = {"dp": middle + owned_k, "tensor": t}
-            place = ag1.at[part, core, owned_r, owned_half]
-            remote(ag1_send.at[part], place, chan_out, device).start()
-        if part == 0:
-            landed(h_all.at[0, pl.ds(0, 3)], HZ)
-            for q in x_near:
-                for n in z_near:
-                    rows = h_all.at[core, n]
-                    remote(rows, rows, HX, {"dp": 2 * q + core}).start()
-            rows = h_all.at[core, pl.ds(column, 4)]
-            remote(rows, rows, HC1, to_core).start()
+
+    def products_sum(part, chan_in, chan_out):
+        @pl.when(core == 1)
+        def _():
+            landed(rs1.at[part], chan_in)
+            for c in range(2):
+                none = jnp.zeros((16, 128), F32)
+                ag1_send[part, c] = summed(none, rs1.at[part, c], 0, N_TP).astype(BF16)
+                for t in tps:
+                    device = {"dp": middle + owned_k, "tensor": t}
+                    place = ag1.at[part, c, owned_r, owned_half]
+                    remote(ag1_send.at[part, c], place, chan_out, device).start()
+
+    products_sum(0, RS1B, AG1B)
+
+    products_sum(1, RS1P, AG1P)
+
+    landed(h_all.at[0, pl.ds(0, 3)], HZ)
+    for q in x_near:
+        for n in z_near:
+            rows = h_all.at[core, n]
+            remote(rows, rows, HX, {"dp": 2 * q + core}).start()
+    rows = h_all.at[core, pl.ds(column, 4)]
+    remote(rows, rows, HC1, to_core).start()
 
     for s, to in enumerate(ys[:-1]):
         for z in range(2):
@@ -372,11 +403,6 @@
             remote(mix_send.at[t], mix_r.at[s, z], MIXY, device).start()
 
     landed(ag1.at[0], AG1B)
-
-    landed(h_all.at[0, pl.ds(0, 12)], HX)
-    for q in x_near:
-        rows = h_all.at[core, pl.ds(4 * lax.div(q, 4), 4)]
-        remote(rows, rows, HC2, to_core).start()
 
     g_down = dot(by_tiles(ag1[0, core]), x[...]) + dot(by_tiles(ag1[0, 1 - core]), x_c[...])
     g_down = g_down.astype(BF16)
@@ -386,14 +412,36 @@
     for s, q in enumerate(chips):
         remote(g_send.at[q], rs2.at[s], RS2, {"dp": 2 * q + core}).start()
 
-    def rows_product(c):
-        part = step_size * adapter_scale * dot_nt(h_all[c].reshape(512, FEAT), g_down)
-        part = part.reshape(N_CHIP, 2, 16, RANK)
-        l_send[c] = jnp.concatenate([part[:, 0], part[:, 1]], axis=2).astype(BF16)
+    def rows_product(xo, c):
+        places = pl.ds(lax.rem(column + 4 * xo, N_CHIP), 4)
+        part = step_size * adapter_scale * dot_nt(h_all[c, places].reshape(128, FEAT), g_down)
+        part = part.reshape(4, 2, 16, RANK)
+        l_send[c, places] = jnp.concatenate([part[:, 0], part[:, 1]], axis=2).astype(BF16)
+
+    def rows_send(xo, zo, half):
+        q = lax.rem(column + 4 * xo, N_CHIP) + lax.rem(z_lo + zo, 4)
+        slot = 2 * (4 * xo + zo) + lax.rem(half + z_hi, 2)
+        device = {"dp": 2 * q + 1, "tensor": N_Y * half + y}
+        place = l_r.at[2 * N_CHIP * core + slot]
+        remote(l_send.at[half, two_along_z(q)], place, LRS, device).start()
+
+    for c in range(2):
+        rows_product(0, c)
         own = step_size * adapter_scale * fold(dot_nt(h_all[c, chip], g_down))
         l_send[c, chip] = (own + h_down[c]).astype(BF16)
-
-    rows_product(core)
+    for zo in (2, 1, 3):
+        rows_send(0, zo, 1 - z_hi)
+        rows_send(0, zo, z_hi)
+    rows_send(0, 0, 1 - z_hi)
+    last = l_send.at[z_hi, two_along_z(chip)]
+
+    @pl.when(core == 0)
+    def _():
+        remote(last, l_r.at[0], LRS, to_core).start()
+
+    @pl.when(core == 1)
+    def _():
+        l_r[2 * N_CHIP] = last[...]
 
     landed(ag1.at[1], AG1P)
 
@@ -404,12 +452,22 @@
     for s, q in enumerate(chips):
         remote(gu_send.at[q], rs2u.at[s], RS2U, {"dp": 2 * q + core}).start()
 
+    landed(h_all.at[0, pl.ds(0, 12)], HX)
+    for q in x_near:
+        rows = h_all.at[core, pl.ds(4 * lax.div(q, 4), 4)]
+        remote(rows, rows, HC2, to_core).start()
+
+    for xo in (2, 1, 3):
+        rows_product(xo, core)
+    for zo in (2, 1, 3, 0):
+        for xo in (2, 1, 3):
+            rows_send(xo, zo, core)
     landed(h_all.at[0, pl.ds(0, 12)], HC2)
-    rows_product(1 - core)
-
-    for s, (q, h) in enumerate(sheet):
-        device = {"dp": 2 * q + core, "tensor": N_Y * h + y}
-        remote(l_send.at[h, two_along_z(q)], l_r.at[s], LRS, device).start()
+    for xo in (2, 1, 3):
+        rows_product(xo, 1 - core)
+    for zo in (2, 1, 3, 0):
+        for xo in (2, 1, 3):
+            rows_send(xo, zo, 1 - core)
 
     landed(base_r, BASEY)
 
@@ -473,14 +531,16 @@
     own_st = packed(top, total)
     own_mix = jnp.concatenate(acc, axis=0)
 
-    landed(l_r, LRS)
-
-    low_send[...] = summed(
-        l_send[z_hi, two_along_z(chip)].astype(F32), l_r, 0, 2 * N_CHIP - 1
-    ).astype(BF16)
-    for t in tps:
-        device = {"dp": middle + z_hi, "tensor": t}
-        remote(low_send, low_r.at[core, y], LOW, device).start()
+    @pl.when(core == 1)
+    def _():
+        landed(l_r.at[pl.ds(0, 4 * N_CHIP - 1)], LRS)
+        for k in range(2):
+            none = jnp.zeros((16, 128), F32)
+            total = summed(none, l_r, 2 * N_CHIP * k, 2 * N_CHIP * (k + 1))
+            low_send[k] = total.astype(BF16)
+        for t in tps:
+            device = {"dp": middle + z_hi, "tensor": t}
+            remote(low_send, low_r.at[y], LOW, device).start()
 
     landed(basez_r, BASEZ)
     base = base + basez_r[...]
@@ -544,9 +604,14 @@
 
     landed(low_r, LOW)
 
-    none = jnp.zeros((16, 128), F32)
-    low_own = unfold(summed(none, low_r.at[core], 0, N_Y)).astype(BF16)
-    low_oth = unfold(summed(none, low_r.at[1 - core], 0, N_Y)).astype(BF16)
+    def total_of(k):
+        acc = low_r[0, k].astype(F32)
+        for n in range(1, N_Y):
+            acc = acc + low_r[n, k].astype(F32)
+        return acc
+
+    low_own = unfold(total_of(core)).astype(BF16)
+    low_oth = unfold(total_of(1 - core)).astype(BF16)
     from_own = adapter_scale * dot(low_own, up_own)
     from_oth = adapter_scale * dot(low_oth, up_oth)
     first = core == 0
@@ -570,35 +635,24 @@
     oa[:, :, 0:HD] = out[:, 0:STEPS].astype(BF16)
     oa[:, :, HD:] = out[:, STEPS:].astype(BF16)
 
-    for ref, chan in (
-        (rs1.at[0], RS1B),
-        (rs1.at[1], RS1P),
-        (ag1.at[0], AG1B),
-        (ag1.at[1], AG1P),
-        (x_c, XC),
-        (wt_c, WC),
-        (h_all.at[0, pl.ds(0, 3)], HZ),
-        (h_all.at[0, pl.ds(0, 12)], HX),
-        (h_all.at[0, pl.ds(0, 4)], HC1),
-        (h_all.at[0, pl.ds(0, 12)], HC2),
-        (l_r, LRS),
-        (rs2u, RS2U),
-        (rs2u, AG2U),
-        (rs2, RS2),
-        (rs2, AG2),
-        (base_r, BASEY),
-        (basez_r, BASEZ),
-        (basep_r, BASEP),
-        (mix_r, MIXY),
-        (st_r, STATY),
-        (mixz_r, MIXZ),
-        (stz_r, STATZ),
-        (low_r, LOW),
-        (ag2_c, DOWNC),
-        (agu_c, UPC),
-        (upx_r, UPX),
-    ):
-        sent(ref, chan)
+    @pl.when(core == 0)
+    def _():
+        sent(SENT_0)
+
+    @pl.when(core == 1)
+    def _():
+        sent(SENT_1)
+
+
+def store(a, b, c, a_h, b_h, c_h, sem):
+    copies = [
+        pltpu.make_async_copy(src, dst, sem.at[n])
+        for n, (src, dst) in enumerate(((a, a_h), (b, b_h), (c, c_h)))
+    ]
+    for copy in copies:
+        copy.start()
+    for copy in copies:
+        copy.wait()
 
 
 def shards(
@@ -633,7 +687,7 @@
         jax.ShapeDtypeStruct((ROWS, STEPS, 2 * HD), BF16),
     )
     vmem = pl.BlockSpec(memory_space=pltpu.VMEM)
-    return pl.pallas_call(
+    results = pl.pallas_call(
         kernel,
         out_shape=out_shape,
         in_specs=[hbm] * 12,
@@ -652,10 +706,10 @@
             pltpu.VMEM((2, 16, ROWS * STEPS, FEAT), BF16),
             pltpu.VMEM((2, 16, 128), F32),
             pltpu.VMEM((2, 16, 16, 128), BF16),
-            pltpu.VMEM((31, 16, 128), BF16),
+            pltpu.VMEM((64, 16, 128), BF16),
             pltpu.VMEM((2, 16, 16, 128), BF16),
-            pltpu.VMEM((2, 16, 16, 128), BF16),
-            pltpu.VMEM((2, 16, 128), BF16),
+            pltpu.VMEM((2, 2, 16, 16, 128), BF16),
+            pltpu.VMEM((2, 2, 16, 128), BF16),
             pltpu.VMEM((2, 2, 4, 2, 16, 128), BF16),
             pltpu.VMEM((16, 16, 128), BF16),
             pltpu.VMEM((15, 16, 128), BF16),
@@ -679,13 +733,14 @@
             pltpu.VMEM((7, 2, 8, 128), F32),
             pltpu.VMEM((8, 128), F32),
             pltpu.VMEM((8, 128), F32),
-            pltpu.VMEM((16, 128), BF16),
-            pltpu.VMEM((2, 8, 16, 128), BF16),
+            pltpu.VMEM((2, 16, 128), BF16),
+            pltpu.VMEM((8, 2, 16, 128), BF16),
             pltpu.VMEM((2, 16, 128), BF16),
             pltpu.VMEM((2, 2, 16, 128), BF16),
             pltpu.VMEM((ROWS, 128, HD), F32),
+            pltpu.VMEM((SENT_1, 2, 128), F32),
             pltpu.SemaphoreType.DMA((12,)),
-            pltpu.SemaphoreType.DMA((N_CHAN,)),
+            pltpu.SemaphoreType.DMA((1,)),
             pltpu.SemaphoreType.DMA((N_CHAN,)),
         ],
         compiler_params=pltpu.CompilerParams(
@@ -697,6 +752,13 @@
             for o in (rewards, group_ids, cache_lengths, *operands)
         )
     )
+    return pl.pallas_call(
+        store,
+        out_shape=out_shape,
+        in_specs=[vmem] * 3,
+        out_specs=(hbm,) * 3,
+        scratch_shapes=[pltpu.SemaphoreType.DMA((3,))],
+    )(*(pltpu.with_memory_space_constraint(r, pltpu.VMEM) for r in results))
 
 
 def solution(mesh):

time: 49.9 us -> 47.9 us (0.960)
  local copies, waits for them, and re-layouts: 1.94 us -> 0 us
    unnamed x3 -> x0, local copies, waits for them, and re-layouts: 1.94 us -> none
    pallas_call x1, Pallas kernels: 47.2 us -> 46.4 us  [shards(): pl.pallas_call(kernel, out_shape=out_shape, in_specs=[hbm] * 12, out_spec...]
    pallas_call x0 -> x1, Pallas kernels: none -> 0.75 us  [shards(): pl.pallas_call(store, out_shape=out_shape, in_specs=[vmem] * 3, out_specs...]
where the time goes in v5:
time: 47.9 us; the launch traced here: 47.8 us
  Pallas kernels  47.2 us (99%)
  between operations  0.64 us (1%)
    pallas_call x1, Pallas kernels, shards(): pl.pallas_call(kernel, out_shape=out_shape, in_specs=[hbm] * 12, out_spec...  46.4 us

profile of v5, /device:TPU:1, one launch (start us, length us, event | category | flops | bytes accessed | tf_op | source)
XLA Modules:
  0.0 47.8 jit_solution(262459572987970095)
XLA Ops:
  0.6 46.4 %shard_map.139 = (f32[2,64,512]{2,1,0:T(8,128)S(1)}, f32[2,64,64]{2,1,0:T(8,128)S(1)}, bf16[8,4,256]{2,1,0:T(4,128)(2,1)S(1)}) custom-call(f32[8]{0:T(128)} %rew_h.1, s32[8]{0:T(128)} %gid_h.1, s32[8]{0:T(128)} %len_h.1, bf16[256,512]{1,0:T(8,128)(2,1)} %x_h.1, bf16[128,256]{1,0:T(8,128)(2,1)} %bitcast.9, f32[2,64,512]{2,1,0:T(8,128)} %down_h.1, ...), custom_call_target="tpu_custom_call" | custom-call | tf_op jit(solution)/shard_map/pallas_call | solution.py:690
  47.1 0.7 %shard_map.140 = (f32[2,64,512]{2,1,0:T(8,128)}, f32[2,64,64]{2,1,0:T(8,128)}, bf16[8,4,256]{2,1,0:T(4,128)(2,1)}) custom-call(f32[2,64,512]{2,1,0:T(8,128)S(1)} %get-tuple-element.6.a, f32[2,64,64]{2,1,0:T(8,128)S(1)} %get-tuple-element.7.b, bf16[8,4,256]{2,1,0:T(4,128)(2,1)S(1)} %get-tuple-element.8.c), custom_call_target="tpu_custom_call" | custom-call | tf_op jit(solution)/shard_map/pallas_call | solution.py:755

commit v6 on v5

--- a/solution.py
+++ b/solution.py
@@ -42,7 +42,9 @@
     HZ,
     HX,
     HC1,
-    HC2,
+    HC2A,
+    HC2B,
+    HC2C,
     LRS,
     RS2,
     RS2U,
@@ -60,7 +62,7 @@
     UPC,
     UPX,
     N_CHAN,
-) = range(27)
+) = range(29)
 
 
 TILE = 4
@@ -240,8 +242,11 @@
         ref = all_sent.at[pl.ds(0, size)]
         pltpu.make_async_copy(ref, ref, send.at[0]).wait()
 
-    def summed(first, ref, start, stop):
-        return lax.fori_loop(start, stop, lambda s, acc: acc + ref[s].astype(F32), first)
+    def summed(ref, start, stop):
+        blocks = [ref[n].astype(F32) for n in range(start, stop)]
+        while len(blocks) > 1:
+            blocks = [sum(blocks[n + 1 : n + 2], blocks[n]) for n in range(0, len(blocks), 2)]
+        return blocks[0]
 
     loads[REW].wait()
     loads[GID].wait()
@@ -316,6 +321,12 @@
             half = slice(RANK * n, RANK * (n + 1))
             base_send[4 * part + n] = jnp.concatenate([new_k[:, half], new_v[:, half]], axis=1)
 
+    for s, to in enumerate(ys[:-1]):
+        for z in range(2):
+            t = N_Y * z + to
+            device = {"tensor": N_Y * z_hi + to}
+            remote(base_send.at[t], base_r.at[s, z], BASEY, device).start()
+
     loads[LEN].wait()
     loads[QRY].wait()
     loads[KEY].wait()
@@ -363,8 +374,7 @@
         def _():
             landed(rs1.at[part], chan_in)
             for c in range(2):
-                none = jnp.zeros((16, 128), F32)
-                ag1_send[part, c] = summed(none, rs1.at[part, c], 0, N_TP).astype(BF16)
+                ag1_send[part, c] = summed(rs1.at[part, c], 0, N_TP).astype(BF16)
                 for t in tps:
                     device = {"dp": middle + owned_k, "tensor": t}
                     place = ag1.at[part, c, owned_r, owned_half]
@@ -381,12 +391,6 @@
             remote(rows, rows, HX, {"dp": 2 * q + core}).start()
     rows = h_all.at[core, pl.ds(column, 4)]
     remote(rows, rows, HC1, to_core).start()
-
-    for s, to in enumerate(ys[:-1]):
-        for z in range(2):
-            t = N_Y * z + to
-            device = {"tensor": N_Y * z_hi + to}
-            remote(base_send.at[t], base_r.at[s, z], BASEY, device).start()
 
     landed(x_c, XC)
     landed(wt_c, WC)
@@ -453,20 +457,19 @@
         remote(gu_send.at[q], rs2u.at[s], RS2U, {"dp": 2 * q + core}).start()
 
     landed(h_all.at[0, pl.ds(0, 12)], HX)
-    for q in x_near:
-        rows = h_all.at[core, pl.ds(4 * lax.div(q, 4), 4)]
-        remote(rows, rows, HC2, to_core).start()
-
-    for xo in (2, 1, 3):
+    far_columns = ((1, HC2A), (2, HC2B), (3, HC2C))
+    for xo, chan in far_columns:
+        rows = h_all.at[core, pl.ds(lax.rem(column + 4 * xo, N_CHIP), 4)]
+        remote(rows, rows, chan, to_core).start()
+
+    for xo, _ in far_columns:
         rows_product(xo, core)
-    for zo in (2, 1, 3, 0):
-        for xo in (2, 1, 3):
+        for zo in (2, 1, 3, 0):
             rows_send(xo, zo, core)
-    landed(h_all.at[0, pl.ds(0, 12)], HC2)
-    for xo in (2, 1, 3):
+    for xo, chan in far_columns:
+        landed(h_all.at[0, pl.ds(0, 4)], chan)
         rows_product(xo, 1 - core)
-    for zo in (2, 1, 3, 0):
-        for xo in (2, 1, 3):
+        for zo in (2, 1, 3, 0):
             rows_send(xo, zo, 1 - core)
 
     landed(base_r, BASEY)
@@ -484,13 +487,13 @@
 
     landed(rs2, RS2)
 
-    ag2[chip] = summed(g_send[chip].astype(F32), rs2, 0, N_CHIP - 1).astype(BF16)
+    ag2[chip] = (g_send[chip].astype(F32) + summed(rs2, 0, N_CHIP - 1)).astype(BF16)
 
     for q in chips:
         remote(ag2.at[chip], ag2.at[chip], AG2, {"dp": 2 * q + core}).start()
 
     landed(rs2u, RS2U)
-    agu[chip] = summed(gu_send[chip], rs2u, 0, N_CHIP - 1)
+    agu[chip] = gu_send[chip] + summed(rs2u, 0, N_CHIP - 1)
     for q in chips:
         remote(agu.at[chip], agu.at[chip], AG2U, {"dp": 2 * q + core}).start()
 
@@ -535,9 +538,7 @@
     def _():
         landed(l_r.at[pl.ds(0, 4 * N_CHIP - 1)], LRS)
         for k in range(2):
-            none = jnp.zeros((16, 128), F32)
-            total = summed(none, l_r, 2 * N_CHIP * k, 2 * N_CHIP * (k + 1))
-            low_send[k] = total.astype(BF16)
+            low_send[k] = summed(l_r, 2 * N_CHIP * k, 2 * N_CHIP * (k + 1)).astype(BF16)
         for t in tps:
             device = {"dp": middle + z_hi, "tensor": t}
             remote(low_send, low_r.at[y], LOW, device).start()
@@ -604,14 +605,8 @@
 
     landed(low_r, LOW)
 
-    def total_of(k):
-        acc = low_r[0, k].astype(F32)
-        for n in range(1, N_Y):
-            acc = acc + low_r[n, k].astype(F32)
-        return acc
-
-    low_own = unfold(total_of(core)).astype(BF16)
-    low_oth = unfold(total_of(1 - core)).astype(BF16)
+    low_own = unfold(summed(low_r.at[:, core], 0, N_Y)).astype(BF16)
+    low_oth = unfold(summed(low_r.at[:, 1 - core], 0, N_Y)).astype(BF16)
     from_own = adapter_scale * dot(low_own, up_own)
     from_oth = adapter_scale * dot(low_oth, up_oth)
     first = core == 0

time: 47.9 us -> 46.7 us (0.975)
  Pallas kernels: 47.2 us -> 46 us
    pallas_call x1, Pallas kernels: 46.4 us -> 45.2 us  [shards(): pl.pallas_call(kernel, out_shape=out_shape, in_specs=[hbm] * 12, out_spec...]
where the time goes in v6:
time: 46.7 us; the launch traced here: 46.6 us
  Pallas kernels  46 us (99%)
  between operations  0.64 us (1%)
    pallas_call x1, Pallas kernels, shards(): pl.pallas_call(kernel, out_shape=out_shape, in_specs=[hbm] * 12, out_spec...  45.2 us

profile of v6, /device:TPU:1, one launch (start us, length us, event | category | flops | bytes accessed | tf_op | source)
XLA Modules:
  0.0 46.6 jit_solution(16442815435437518054)
XLA Ops:
  0.6 45.2 %shard_map.139 = (f32[2,64,512]{2,1,0:T(8,128)S(1)}, f32[2,64,64]{2,1,0:T(8,128)S(1)}, bf16[8,4,256]{2,1,0:T(4,128)(2,1)S(1)}) custom-call(f32[8]{0:T(128)} %rew_h.1, s32[8]{0:T(128)} %gid_h.1, s32[8]{0:T(128)} %len_h.1, bf16[256,512]{1,0:T(8,128)(2,1)} %x_h.1, bf16[128,256]{1,0:T(8,128)(2,1)} %bitcast.9, f32[2,64,512]{2,1,0:T(8,128)} %down_h.1, ...), custom_call_target="tpu_custom_call" | custom-call | tf_op jit(solution)/shard_map/pallas_call | solution.py:685
  45.9 0.7 %shard_map.140 = (f32[2,64,512]{2,1,0:T(8,128)}, f32[2,64,64]{2,1,0:T(8,128)}, bf16[8,4,256]{2,1,0:T(4,128)(2,1)}) custom-call(f32[2,64,512]{2,1,0:T(8,128)S(1)} %get-tuple-element.6.a, f32[2,64,64]{2,1,0:T(8,128)S(1)} %get-tuple-element.7.b, bf16[8,4,256]{2,1,0:T(4,128)(2,1)S(1)} %get-tuple-element.8.c), custom_call_target="tpu_custom_call" | custom-call | tf_op jit(solution)/shard_map/pallas_call | solution.py:750

commit v7 on v6

--- a/solution.py
+++ b/solution.py
@@ -40,6 +40,9 @@
     XC,
     WC,
     HZ,
+    HZ_1,
+    HZ_2,
+    HZ_3,
     HX,
     HC1,
     HC2A,
@@ -62,7 +65,7 @@
     UPC,
     UPX,
     N_CHAN,
-) = range(29)
+) = range(32)
 
 
 TILE = 4
@@ -308,7 +311,7 @@
     h_all[core, chip] = hid_b
     rows = h_all.at[core, chip]
     for q in z_near:
-        remote(rows, rows, HZ, {"dp": 2 * q + core}).start()
+        remote(rows, rows, HZ + z_lo, {"dp": 2 * q + core}).start()
     for q in x_near:
         remote(rows, rows, HX, {"dp": 2 * q + core}).start()
 
@@ -382,13 +385,23 @@
 
     products_sum(0, RS1B, AG1B)
 
+    def pass_on(z):
+        rows = h_all.at[core, column + z]
+        landed(rows, HZ + z)
+        for q in x_near:
+            remote(rows, rows, HX, {"dp": 2 * q + core}).start()
+
+    column_order = (
+        jnp.where(z_lo == 0, 2, 0),
+        jnp.where(lax.rem(z_lo, 2) == 1, 2, 3),
+        jnp.where(z_lo == 1, 3, 1),
+    )
+    pass_on(column_order[0])
+    pass_on(column_order[1])
+
     products_sum(1, RS1P, AG1P)
 
-    landed(h_all.at[0, pl.ds(0, 3)], HZ)
-    for q in x_near:
-        for n in z_near:
-            rows = h_all.at[core, n]
-            remote(rows, rows, HX, {"dp": 2 * q + core}).start()
+    pass_on(column_order[2])
     rows = h_all.at[core, pl.ds(column, 4)]
     remote(rows, rows, HC1, to_core).start()
 

time: 46.7 us -> 46.1 us (0.987)
  Pallas kernels: 46 us -> 45.3 us
    pallas_call x1, Pallas kernels: 45.2 us -> 44.6 us  [shards(): pl.pallas_call(kernel, out_shape=out_shape, in_specs=[hbm] * 12, out_spec...]
where the time goes in v7:
time: 46.1 us; the launch traced here: 46 us
  Pallas kernels  45.3 us (98%)
  between operations  0.64 us (1%)
    pallas_call x1, Pallas kernels, shards(): pl.pallas_call(kernel, out_shape=out_shape, in_specs=[hbm] * 12, out_spec...  44.6 us

profile of v7, /device:TPU:1, one launch (start us, length us, event | category | flops | bytes accessed | tf_op | source)
XLA Modules:
  0.0 46.0 jit_solution(5950706328613137670)
XLA Ops:
  0.6 44.6 %shard_map.139 = (f32[2,64,512]{2,1,0:T(8,128)S(1)}, f32[2,64,64]{2,1,0:T(8,128)S(1)}, bf16[8,4,256]{2,1,0:T(4,128)(2,1)S(1)}) custom-call(f32[8]{0:T(128)} %rew_h.1, s32[8]{0:T(128)} %gid_h.1, s32[8]{0:T(128)} %len_h.1, bf16[256,512]{1,0:T(8,128)(2,1)} %x_h.1, bf16[128,256]{1,0:T(8,128)(2,1)} %bitcast.9, f32[2,64,512]{2,1,0:T(8,128)} %down_h.1, ...), custom_call_target="tpu_custom_call" | custom-call | tf_op jit(solution)/shard_map/pallas_call | solution.py:698
  45.2 0.7 %shard_map.140 = (f32[2,64,512]{2,1,0:T(8,128)}, f32[2,64,64]{2,1,0:T(8,128)}, bf16[8,4,256]{2,1,0:T(4,128)(2,1)}) custom-call(f32[2,64,512]{2,1,0:T(8,128)S(1)} %get-tuple-element.6.a, f32[2,64,64]{2,1,0:T(8,128)S(1)} %get-tuple-element.7.b, bf16[8,4,256]{2,1,0:T(4,128)(2,1)S(1)} %get-tuple-element.8.c), custom_call_target="tpu_custom_call" | custom-call | tf_op jit(solution)/shard_map/pallas_call | solution.py:763
